TPU v7x, 32 devices: a whole 2x2x4 slice. The times are simulated.
32 devices in a mesh: seq: 32 (over z, y, x, core).
Axes of the slice: x: 2, y: 2, z: 4, core: 2. Of those that a mesh axis runs over, the one named last changes fastest.
Arguments:
- hidden: bfloat16 [4096, 768], P('seq'), may hold values from -6 to 6
- condition: float32 [6, 768], replicated, may hold values from -6 to 6
- seq_lengths: int32 [6], replicated, may hold values from 1 to 4032, as said below
- w_mod: bfloat16 [768, 2304], replicated, may hold values from -0.21875 to 0.21875
- b_mod: float32 [2304], replicated, may hold values from -2 to 2
- w_in: bfloat16 [768, 3072], replicated, may hold values from -0.21875 to 0.21875
- conv_w: float32 [2, 4, 1536], replicated, may hold values from -3 to 3
- conv_b: float32 [2, 1536], replicated, may hold values from -0.5 to 0.5
- w_x: bfloat16 [2, 1536, 80], replicated, may hold values from -0.15625 to 0.15625
- w_dt: bfloat16 [2, 48, 1536], replicated, may hold values from -0.875 to 0.875
- dt_bias: float32 [2, 1536], replicated, may hold values from -6.5 to -2.3
- a_log: float32 [2, 16, 1536], replicated, may hold values from -9 to 1
- d_skip: float32 [2, 1536], replicated, may hold values from 0.5 to 1.5
- w_out: bfloat16 [1536, 768], replicated, may hold values from -0.4375 to 0.4375
- grad_out: bfloat16 [4096, 768], P('seq'), may hold values from -6 to 6
Outputs:
- output: bfloat16 [4096, 768], P('seq')
- grad_hidden: float32 [4096, 768], P('seq')
- grad_w_mod: float32 [768, 2304], P('seq')
- grad_b_mod: float32 [2304], P('seq')
- grad_w_in: float32 [768, 3072], P('seq')
- grad_conv_w: float32 [2, 4, 1536], P(None, None, 'seq')
- grad_conv_b: float32 [2, 1536], P(None, 'seq')
- grad_w_x: float32 [2, 1536, 80], P(None, 'seq')
- grad_w_dt: float32 [2, 48, 1536], P(None, None, 'seq')
- grad_dt_bias: float32 [2, 1536], P(None, 'seq')
- grad_a_log: float32 [2, 16, 1536], P(None, None, 'seq')
- grad_d_skip: float32 [2, 1536], P(None, 'seq')
- grad_w_out: float32 [1536, 768], P('seq')
Inputs may be any that keep to these rules, and one draw needn't show every extreme that they name: `seq_lengths`: the sequences lie one after another from token 0 and are followed by one or more padding tokens. One of them, which one varies, is a high-resolution image's patch tokens with 4032 tokens; each other one has at most (63) // 5.
All inputs are finite; a program needn't handle non-finite values.
Results may differ from a plain program's by a relative error of at most 0.0097.
Values may be sent and summed in bfloat16 or wider, within the bound.
A program may use at most 192 MiB of HBM per device.

v0:
```python
import functools

import jax
import jax.numpy as jnp
from jax import lax
from jax.experimental import pallas as pl
from jax.experimental.pallas import tpu as pltpu
from jax.sharding import PartitionSpec as P

EPSILON = 1e-06
HIGHEST = lax.Precision.HIGHEST
MESH = pl.DeviceIdType.MESH
LANES = 128
LOG2E = 1.4426950408889634
LN2 = 0.6931471805599453
CUT_STEP = 1e9
PLANE = 8
RIM = 8
CHUNK = 16
MIB = 1024 * 1024


def segment_ids(positions, bounds):
    return jnp.sum((positions[:, None] >= bounds[None, :]).astype(jnp.int32), axis=1) - 1


def silu_slope(values):
    sigma = jax.nn.sigmoid(values)
    return sigma * (1.0 + values * (1.0 - sigma))


def contract_rows(left, right):
    return lax.dot_general(
        left, right, (((0,), (0,)), ((), ())), preferred_element_type=jnp.float32
    )


def contract_cols(left, right):
    return lax.dot_general(
        left, right, (((1,), (1,)), ((), ())), preferred_element_type=jnp.float32
    )


def tile_of(c):
    return pl.ds(c * LANES, LANES)


def row_of(ref, first, j, c):
    eight = pl.ds(pl.multiple_of(first + j // 8 * 8, 8), 8)
    return ref.at[eight, tile_of(c)][j % 8 : j % 8 + 1, :]


def summary_kernel(
    step0, step1, drv0, drv1, seed, in0, in1, out0, out1, rate, sums
):
    tokens = step0.shape[0]
    tiles = step0.shape[1] // LANES
    dirs = ((step0, drv0, in0, out0), (step1, drv1, in1, out1))

    def group(i, carry):
        carry = list(carry)
        for k in range(8):
            for d, (step, drv, inc, outc) in enumerate(dirs):
                first = pl.multiple_of((i if d == 0 else tokens // 8 - 1 - i) * 8, 8)
                j = k if d == 0 else 7 - k
                in_row = inc[first + j]
                out_row = outc[first + j]
                for c in range(tiles):
                    state, decay, adj = carry[d * tiles + c]
                    now = jnp.exp2(row_of(step, first, j, c) * rate[d, :, tile_of(c)])
                    state = now * state + in_row * row_of(drv, first, j, c)
                    decay = decay * now
                    adj = adj + decay * (out_row * row_of(seed, first, j, c))
                    carry[d * tiles + c] = (state, decay, adj)
        return tuple(carry)

    zero = jnp.zeros((rate.shape[1], LANES), jnp.float32)
    one = jnp.ones((rate.shape[1], LANES), jnp.float32)
    carry = lax.fori_loop(0, tokens // 8, group, tuple((zero, one, zero) for _ in range(2 * tiles)))
    for d in range(2):
        for c in range(tiles):
            state, decay, adj = carry[d * tiles + c]
            down, up = (adj, state) if d == 0 else (state, adj)
            sums[d, c, 0] = down
            sums[d, c, 1] = decay
            sums[d, c, 2] = up


def summaries(steps, drvs, seed, ins, outs, rate):
    tokens, width = seed.shape
    states = rate.shape[1]
    cols = 256 if width % 256 == 0 else LANES
    rows = pl.BlockSpec((tokens, cols), lambda b: (0, b))
    coef = pl.BlockSpec((tokens, states, LANES), lambda b: (0, 0, 0))
    return pl.pallas_call(
        summary_kernel,
        grid=(width // cols,),
        in_specs=[rows] * 5 + [coef] * 4 + [pl.BlockSpec((2, states, cols), lambda b: (0, 0, b))],
        out_specs=pl.BlockSpec((2, cols // LANES, 3, states, LANES), lambda b: (0, b, 0, 0, 0)),
        out_shape=jax.ShapeDtypeStruct((2, width // LANES, 3, states, LANES), jnp.float32),
        compiler_params=pltpu.CompilerParams(vmem_limit_bytes=48 * MIB),
        name="summaries",
    )(steps[0], steps[1], drvs[0], drvs[1], seed, ins[0], ins[1], outs[0], outs[1], rate)


def carry_kernel(
    count, sums, entering, got, total, others, back, send1, recv1, send2, recv2, send3, recv3
):
    groups = count // PLANE
    me = lax.axis_index("seq")
    mine = lax.rem(me, PLANE)
    level = me // PLANE
    base = level * PLANE
    share = sums.shape[1]

    barrier = pltpu.get_barrier_semaphore()
    for k in range(1, PLANE):
        pl.semaphore_signal(
            barrier, inc=1, device_id=(base + lax.rem(mine + k, PLANE),), device_id_type=MESH
        )
    for k in range(1, groups):
        pl.semaphore_signal(
            barrier,
            inc=1,
            device_id=(lax.rem(level + k, groups) * PLANE + mine,),
            device_id_type=MESH,
        )
    pl.semaphore_wait(barrier, PLANE - 1 + groups - 1)

    first = []
    for k in range(1, PLANE):
        peer = lax.rem(mine + k, PLANE)
        copy = pltpu.make_async_remote_copy(
            src_ref=sums.at[peer],
            dst_ref=got.at[mine],
            send_sem=send1.at[k],
            recv_sem=recv1.at[k],
            device_id=(base + peer,),
            device_id_type=MESH,
        )
        copy.start()
        first.append(copy)
    got[mine] = sums[mine]
    others[level] = jnp.zeros(others.shape[1:], jnp.float32)
    for copy in first:
        copy.wait_recv()

    block = sums.shape[1:2] + sums.shape[3:]
    up = jnp.zeros(block, jnp.float32)
    decay = jnp.ones(block, jnp.float32)
    for j in range(PLANE):
        up = got[j, :, 1] * up + got[j, :, 2]
        decay = decay * got[j, :, 1]
    down = jnp.zeros(block, jnp.float32)
    for j in reversed(range(PLANE)):
        down = got[j, :, 1] * down + got[j, :, 0]
    total[0] = down
    total[1] = decay
    total[2] = up

    second = []
    for k in range(1, groups):
        other = lax.rem(level + k, groups)
        start = jnp.where(other > level, 1, 0)
        copy = pltpu.make_async_remote_copy(
            src_ref=total.at[pl.ds(start, 2)],
            dst_ref=others.at[level],
            send_sem=send2.at[k],
            recv_sem=recv2.at[k],
            device_id=(other * PLANE + mine,),
            device_id_type=MESH,
        )
        copy.start()
        second.append(copy)
    for copy in second:
        copy.wait_recv()

    up = jnp.zeros(block, jnp.float32)
    for g in range(groups):
        up = jnp.where(g < level, others[g, 0] * up + others[g, 1], up)
    down = jnp.zeros(block, jnp.float32)
    for g in reversed(range(groups)):
        down = jnp.where(g > level, others[g, 1] * down + others[g, 0], down)
    for j in range(PLANE):
        back[j, :, 0] = up
        up = got[j, :, 1] * up + got[j, :, 2]
    for j in reversed(range(PLANE)):
        back[j, :, 1] = down
        down = got[j, :, 1] * down + got[j, :, 0]

    third = []
    here = pl.ds(mine * share, share)
    for k in range(1, PLANE):
        peer = lax.rem(mine + k, PLANE)
        copy = pltpu.make_async_remote_copy(
            src_ref=back.at[peer],
            dst_ref=entering.at[here],
            send_sem=send3.at[k],
            recv_sem=recv3.at[k],
            device_id=(base + peer,),
            device_id_type=MESH,
        )
        copy.start()
        third.append(copy)
    entering[here] = back[mine]
    for copy in third:
        copy.wait_recv()
    for copy in first + second + third:
        copy.wait_send()


def carries(sums, count):
    _, tiles, _, states, _ = sums.shape
    share = 2 * tiles // PLANE
    groups = count // PLANE
    stacked = sums.reshape(PLANE, share, 3, states, LANES)
    vmem = pl.BlockSpec(memory_space=pltpu.VMEM)
    entering = pl.pallas_call(
        functools.partial(carry_kernel, count),
        in_specs=[vmem],
        out_specs=vmem,
        out_shape=jax.ShapeDtypeStruct((2 * tiles, 2, states, LANES), jnp.float32),
        scratch_shapes=[
            pltpu.VMEM((PLANE, share, 3, states, LANES), jnp.float32),
            pltpu.VMEM((3, share, states, LANES), jnp.float32),
            pltpu.VMEM((groups, 2, share, states, LANES), jnp.float32),
            pltpu.VMEM((PLANE, share, 2, states, LANES), jnp.float32),
            pltpu.SemaphoreType.DMA((PLANE,)),
            pltpu.SemaphoreType.DMA((PLANE,)),
            pltpu.SemaphoreType.DMA((groups,)),
            pltpu.SemaphoreType.DMA((groups,)),
            pltpu.SemaphoreType.DMA((PLANE,)),
            pltpu.SemaphoreType.DMA((PLANE,)),
        ],
        compiler_params=pltpu.CompilerParams(
            collective_id=0, has_side_effects=True, vmem_limit_bytes=32 * MIB
        ),
        name="carries",
    )(stacked)
    return entering.reshape(2, tiles, 2, states, LANES)


def scan_kernel(
    step0,
    step1,
    drv0,
    drv1,
    seed,
    in0,
    in1,
    out0,
    out1,
    in_blk,
    out_blk,
    ones_blk,
    rate,
    entering,
    y0,
    y1,
    dec0,
    dec1,
    dg0,
    dg1,
    in_grad,
    out_grad,
    rate_grad,
    kept_decay,
    kept_held,
    rows_a,
    rows_b,
    rows_c,
    rows_d,
):
    tokens = step0.shape[0]
    tiles = step0.shape[1] // LANES
    states = rate.shape[1]
    chunks = tokens // CHUNK
    steps, drvs = (step0, step1), (drv0, drv1)
    ins, outs = (in0, in1), (out0, out1)
    ys, decs, dgs = (y0, y1), (dec0, dec1), (dg0, dg1)

    @pl.when(pl.program_id(0) == 0)
    def _():
        in_grad[...] = jnp.zeros_like(in_grad)
        out_grad[...] = jnp.zeros_like(out_grad)

    def forward(i, carry):
        carry = list(carry)
        for d in range(2):
            first = pl.multiple_of((i if d == 0 else chunks - 1 - i) * CHUNK, CHUNK)
            kept = (rows_a, rows_b)[d]
            for k in range(CHUNK):
                j = k if d == 0 else CHUNK - 1 - k
                t = first + j
                in_row = ins[d][t]
                for c in range(tiles):
                    lanes = tile_of(c)
                    now = jnp.exp2(row_of(steps[d], first, j, c) * rate[d, :, lanes])
                    held = now * carry[d * tiles + c]
                    state = held + in_row * row_of(drvs[d], first, j, c)
                    kept_decay[d, t, :, lanes] = now
                    kept_held[d, t, :, lanes] = held
                    kept[j * states : (j + 1) * states, lanes] = state.astype(jnp.bfloat16)
                    carry[d * tiles + c] = state
            here = pl.ds(first, CHUNK)
            block = kept[...]
            ys[d][here, :] = jnp.dot(
                out_blk[d, here, :], block, preferred_element_type=jnp.float32
            )
            out_grad[d, here, :] += contract_cols(seed[here, :].astype(jnp.bfloat16), block)
        return tuple(carry)

    start = tuple(entering[d, c, d] for d in range(2) for c in range(tiles))
    lax.fori_loop(0, chunks, forward, start)

    def backward(i, carry):
        carry = list(carry)
        for d in range(2):
            first = pl.multiple_of((chunks - 1 - i if d == 0 else i) * CHUNK, CHUNK)
            kept = (rows_a, rows_b)[d]
            grads = (rows_c, rows_d)[d]
            for k in range(CHUNK):
                j = CHUNK - 1 - k if d == 0 else k
                t = first + j
                out_row = outs[d][t]
                for c in range(tiles):
                    lanes = tile_of(c)
                    coming, total = carry[d * tiles + c]
                    step = row_of(steps[d], first, j, c)
                    adj = out_row * row_of(seed, first, j, c) + coming
                    coming = kept_decay[d, t, :, lanes] * adj
                    slope = adj * kept_held[d, t, :, lanes] * rate[d, :, lanes]
                    total = total + slope * step
                    kept[j * states : (j + 1) * states, lanes] = adj.astype(jnp.bfloat16)
                    grads[j * states : (j + 1) * states, lanes] = slope.astype(jnp.bfloat16)
                    carry[d * tiles + c] = (coming, total)
            here = pl.ds(first, CHUNK)
            block = kept[...]
            dgs[d][here, :] = jnp.dot(
                in_blk[d, here, :], block, preferred_element_type=jnp.float32
            )
            in_grad[d, here, :] += contract_cols(drvs[d][here, :].astype(jnp.bfloat16), block)
            decs[d][here, :] = (
                jnp.dot(ones_blk[...], grads[...], preferred_element_type=jnp.float32) * LN2
            )
        return tuple(carry)

    zero = jnp.zeros((states, LANES), jnp.float32)
    start = tuple((entering[d, c, 1 - d], zero) for d in range(2) for c in range(tiles))
    carry = lax.fori_loop(0, chunks, backward, start)
    for d in range(2):
        for c in range(tiles):
            rate_grad[d, :, c * LANES : (c + 1) * LANES] = carry[d * tiles + c][1] * LN2


def scans(steps, drvs, seed, ins, outs, in_blk, out_blk, ones_blk, rate, entering):
    tokens, width = seed.shape
    states = rate.shape[1]
    cols = 256 if width % 256 == 0 else LANES
    tiles = cols // LANES
    wide = CHUNK * states
    rows = pl.BlockSpec((tokens, cols), lambda b: (0, b))
    coef = pl.BlockSpec((tokens, states, LANES), lambda b: (0, 0, 0))
    diag = pl.BlockSpec((2, tokens, wide), lambda b: (0, 0, 0))
    by_state = pl.BlockSpec((2, states, cols), lambda b: (0, 0, b))
    full = jax.ShapeDtypeStruct((tokens, width), jnp.float32)
    diag_out = jax.ShapeDtypeStruct((2, tokens, wide), jnp.float32)
    return pl.pallas_call(
        scan_kernel,
        grid=(width // cols,),
        in_specs=[rows] * 5
        + [coef] * 4
        + [diag, diag, pl.BlockSpec((CHUNK, wide), lambda b: (0, 0)), by_state]
        + [pl.BlockSpec((2, tiles, 2, states, LANES), lambda b: (0, b, 0, 0, 0))],
        out_specs=[rows] * 6 + [diag, diag, by_state],
        out_shape=[full] * 6
        + [diag_out, diag_out, jax.ShapeDtypeStruct((2, states, width), jnp.float32)],
        scratch_shapes=[
            pltpu.VMEM((2, tokens, states, cols), jnp.float32),
            pltpu.VMEM((2, tokens, states, cols), jnp.float32),
        ]
        + [pltpu.VMEM((wide, cols), jnp.bfloat16)] * 4,
        compiler_params=pltpu.CompilerParams(vmem_limit_bytes=48 * MIB),
        name="scans",
    )(
        steps[0],
        steps[1],
        drvs[0],
        drvs[1],
        seed,
        ins[0],
        ins[1],
        outs[0],
        outs[1],
        in_blk,
        out_blk,
        ones_blk,
        rate,
        entering,
    )


def reduce_kernel(
    count,
    part_a,
    part_b,
    mod,
    rim,
    out_a,
    out_b,
    out_mod,
    out_rim,
    a1,
    b1,
    a2,
    b2,
    a3,
    b3,
    a4,
    b4,
    m1,
    m2,
    m3,
    m4,
    send,
    recv,
    send_far,
    recv_far,
):
    groups = count // PLANE
    me = lax.axis_index("seq")
    bit0 = lax.rem(me, 2)
    bit1 = lax.rem(me // 2, 2)
    bit2 = lax.rem(me // 4, 2)
    level = me // PLANE
    low = lax.rem(me, PLANE)
    flip0 = me + 1 - 2 * bit0
    flip1 = me + 2 - 4 * bit1
    flip2 = me + 4 - 8 * bit2
    left = lax.rem(me + count - 1, count)
    right = lax.rem(me + 1, count)

    def other(k):
        return lax.rem(level + k, groups)

    barrier = pltpu.get_barrier_semaphore()
    peers = [flip0, flip1, flip2, left, right] + [other(k) * PLANE + low for k in range(1, groups)]
    for peer in peers:
        pl.semaphore_signal(barrier, inc=1, device_id=(peer,), device_id_type=MESH)
    pl.semaphore_wait(barrier, len(peers))

    started = []

    def push(src, dst, slot, peer, sems=None):
        sends, recvs = sems or (send, recv)
        copy = pltpu.make_async_remote_copy(
            src_ref=src,
            dst_ref=dst,
            send_sem=sends.at[slot],
            recv_sem=recvs.at[slot],
            device_id=(peer,),
            device_id_type=MESH,
        )
        copy.start()
        started.append(copy)
        return copy

    def add(into, own, first):
        def one(i, none):
            into[i] = (
                into[i].astype(jnp.float32) + own[first + i].astype(jnp.float32)
            ).astype(into.dtype)
            return none

        lax.fori_loop(0, into.shape[0], one, 0)

    edge_l = push(rim.at[pl.ds(0, RIM)], out_rim.at[pl.ds(RIM, RIM)], 0, left)
    edge_r = push(rim.at[pl.ds(RIM, RIM)], out_rim.at[pl.ds(0, RIM)], 1, right)

    got_m = push(mod, m1, 2, flip0)
    got_a = push(part_a.at[1 - bit0], a1, 3, flip0)
    got_b = push(part_b.at[1 - bit0], b1, 4, flip0)
    got_m.wait_recv()
    m1[...] += mod[...]
    half = 2 * groups
    got_a.wait_recv()
    add(a1, part_a.at[bit0], 0)
    got_m = push(m1, m2, 5, flip1)
    got_a = push(a1.at[pl.ds((1 - bit1) * half, half)], a2, 6, flip1)
    got_b.wait_recv()
    add(b1, part_b.at[bit0], 0)
    got_b = push(b1.at[pl.ds((1 - bit2) * half, half)], b2, 7, flip2)
    got_m.wait_recv()
    m2[...] += m1[...]
    got_m = push(m2, m3, 8, flip2)
    got_a.wait_recv()
    add(a2, a1, bit1 * half)
    got_a = push(a2.at[pl.ds((1 - bit2) * groups, groups)], a3, 9, flip2)
    got_b.wait_recv()
    add(b2, b1, bit2 * half)
    got_b = push(b2.at[pl.ds((1 - bit1) * groups, groups)], b3, 10, flip1)
    got_m.wait_recv()
    m3[...] += m2[...]
    far = (send_far, recv_far)
    last = []
    for k in range(1, groups):
        last.append(push(m3, m4.at[level], 3 * k, other(k) * PLANE + low, far))
    got_a.wait_recv()
    add(a3, a2, bit2 * groups)
    for k in range(1, groups):
        last.append(
            push(a3.at[other(k)], a4.at[level], 3 * k + 1, other(k) * PLANE + low, far)
        )
    got_b.wait_recv()
    add(b3, b2, bit1 * groups)
    for k in range(1, groups):
        last.append(
            push(b3.at[other(k)], b4.at[level], 3 * k + 2, other(k) * PLANE + low, far)
        )
    a4[level] = a3[level]
    b4[level] = b3[level]
    m4[level] = m3[...]
    for copy in last:
        copy.wait_recv()
    edge_l.wait_recv()
    edge_r.wait_recv()
    for into, held in ((out_a, a4), (out_b, b4), (out_mod, m4)):
        total = held[0].astype(jnp.float32)
        for g in range(1, groups):
            total = total + held[g].astype(jnp.float32)
        into[...] = total
    for copy in started:
        copy.wait_send()


def reduce_shares(part_a, part_b, mod, rim, count):
    groups = count // PLANE
    vmem = pl.BlockSpec(memory_space=pltpu.VMEM)
    rows, cols_a = part_a.shape[-2:]
    cols_b = part_b.shape[-1]

    def slots(number):
        return [
            pltpu.VMEM((number, rows, cols_a), jnp.bfloat16),
            pltpu.VMEM((number, rows, cols_b), jnp.bfloat16),
        ]

    return pl.pallas_call(
        functools.partial(reduce_kernel, count),
        in_specs=[vmem] * 4,
        out_specs=[vmem] * 4,
        out_shape=[
            jax.ShapeDtypeStruct((rows, cols_a), jnp.float32),
            jax.ShapeDtypeStruct((rows, cols_b), jnp.float32),
            jax.ShapeDtypeStruct(mod.shape, jnp.float32),
            jax.ShapeDtypeStruct(rim.shape, jnp.float32),
        ],
        scratch_shapes=slots(4 * groups)
        + slots(2 * groups)
        + slots(groups)
        + slots(groups)
        + [pltpu.VMEM(mod.shape, jnp.float32)] * 3
        + [
            pltpu.VMEM((groups,) + mod.shape, jnp.float32),
            pltpu.SemaphoreType.DMA((11,)),
            pltpu.SemaphoreType.DMA((11,)),
            pltpu.SemaphoreType.DMA((3 * groups,)),
            pltpu.SemaphoreType.DMA((3 * groups,)),
        ],
        compiler_params=pltpu.CompilerParams(
            collective_id=1, has_side_effects=True, vmem_limit_bytes=48 * MIB
        ),
        name="reduce_shares",
    )(part_a, part_b, mod, rim)


def on_device(
    count,
    hidden,
    condition,
    seq_lengths,
    w_mod,
    b_mod,
    w_in,
    conv_w,
    conv_b,
    w_x,
    w_dt,
    dt_bias,
    a_log,
    d_skip,
    w_out,
    grad_out,
):
    tokens, model = hidden.shape
    seq_count = condition.shape[0]
    inner = w_in.shape[1] // 2
    rank = w_dt.shape[1]
    states = a_log.shape[1]
    taps = conv_w.shape[1]
    groups = count // PLANE
    me = lax.axis_index("seq")
    first_row = me * tokens

    below = lax.ppermute(hidden[-RIM:], "seq", [(i, i + 1) for i in range(count - 1)])
    above = lax.ppermute(hidden[:RIM], "seq", [(i + 1, i) for i in range(count - 1)])
    own = slice(RIM, RIM + tokens)
    positions = first_row - RIM + jnp.arange(tokens + 2 * RIM, dtype=jnp.int32)
    bounds = jnp.concatenate([jnp.zeros((1,), jnp.int32), jnp.cumsum(seq_lengths)])
    wide_segment = segment_ids(positions, bounds)
    segment = wide_segment[own]

    def same(offset):
        return wide_segment[RIM + offset : RIM + offset + tokens] == segment

    onehot = (wide_segment[:, None] == jnp.arange(seq_count, dtype=jnp.int32)[None, :]).astype(
        jnp.float32
    )
    cond_act = jax.nn.silu(condition).astype(jnp.bfloat16)
    modulation = jnp.dot(cond_act, w_mod, preferred_element_type=jnp.float32) + b_mod[None, :]
    mod_rows = jnp.dot(onehot, modulation, precision=HIGHEST, preferred_element_type=jnp.float32)
    shift_rows = mod_rows[:, :model]
    scale_rows = mod_rows[:, model : 2 * model]
    gate_rows = mod_rows[own, 2 * model :]

    x_wide = jnp.concatenate([below, hidden, above], axis=0).astype(jnp.float32)
    row_mean = jnp.mean(x_wide, axis=1, keepdims=True)
    centered = x_wide - row_mean
    rescale = lax.rsqrt(jnp.mean(centered * centered, axis=1, keepdims=True) + EPSILON)
    normed = centered * rescale
    mixer_in = (normed * (1.0 + scale_rows) + shift_rows).astype(jnp.bfloat16)
    conv_wide = (
        jnp.dot(mixer_in, w_in[:, :inner], preferred_element_type=jnp.float32)
        .astype(jnp.bfloat16)
        .astype(jnp.float32)
    )
    gate_branch = jnp.dot(mixer_in[own], w_in[:, inner:], preferred_element_type=jnp.float32)

    cotangent = grad_out.astype(jnp.float32)
    branch_grad = (cotangent * gate_rows).astype(jnp.bfloat16)
    gated_grad = contract_cols(branch_grad, w_out)
    gate_silu = jax.nn.silu(gate_branch)
    mixed_grad = gated_grad * gate_silu

    saved = []
    for d in range(2):
        conv_sum = conv_b[d][None, :]
        for k in range(taps):
            offset = k - (taps - 1) if d == 0 else taps - 1 - k
            conv_sum = conv_sum + conv_w[d, k][None, :] * conv_wide[
                RIM + offset : RIM + offset + tokens
            ] * same(offset).astype(jnp.float32)[:, None]
        active = jax.nn.silu(conv_sum).astype(jnp.bfloat16)
        projection = jnp.dot(active, w_x[d], preferred_element_type=jnp.float32)
        rank_low = projection[:, :rank].astype(jnp.bfloat16)
        in_coef = projection[:, rank : rank + states]
        out_coef = projection[:, rank + states :]
        logit = (
            jnp.dot(rank_low, w_dt[d], preferred_element_type=jnp.float32) + dt_bias[d][None, :]
        )
        step = jax.nn.softplus(logit)
        keep = same(-1) if d == 0 else same(1)
        masked = jnp.where(keep[:, None], step, CUT_STEP)
        driven = step * active.astype(jnp.float32)
        saved.append((conv_sum, active, rank_low, in_coef, out_coef, logit, step, masked, driven))

    def spread(coef):
        return jnp.broadcast_to(coef[:, :, None], (tokens, states, LANES))

    place = jnp.arange(tokens, dtype=jnp.int32) % CHUNK
    on_diag = (place[:, None] == jnp.arange(CHUNK, dtype=jnp.int32)[None, :]).astype(jnp.float32)

    def block_diag(coef):
        wide = on_diag[:, :, None] * coef[:, None, :]
        return wide.reshape(tokens, CHUNK * states).astype(jnp.bfloat16)

    rate = -jnp.exp(a_log)
    steps = [s[7] for s in saved]
    drvs = [s[8] for s in saved]
    ins = [spread(s[3]) for s in saved]
    outs = [spread(s[4]) for s in saved]
    in_blk = jnp.stack([block_diag(s[3]) for s in saved])
    out_blk = jnp.stack([block_diag(s[4]) for s in saved])
    ones_blk = block_diag(jnp.ones((tokens, states), jnp.float32))[:CHUNK]
    fast_rate = rate * LOG2E
    sums = summaries(steps, drvs, mixed_grad, ins, outs, fast_rate)
    entering = carries(sums, count)
    y0, y1, dec0, dec1, dg0, dg1, in_acc, out_acc, rate_grad = scans(
        steps, drvs, mixed_grad, ins, outs, in_blk, out_blk, ones_blk, fast_rate, entering
    )
    in_grads = jnp.sum(in_acc.reshape(2, tokens, CHUNK, states) * on_diag[None, :, :, None], axis=2)
    out_grads = jnp.sum(
        out_acc.reshape(2, tokens, CHUNK, states) * on_diag[None, :, :, None], axis=2
    )

    mixed = y0 + y1
    for d in range(2):
        mixed = mixed + d_skip[d][None, :] * saved[d][1].astype(jnp.float32)
    gated = (mixed * gate_silu).astype(jnp.bfloat16)
    branch = jnp.dot(gated, w_out, preferred_element_type=jnp.float32)
    output = (x_wide[own] + gate_rows * branch).astype(jnp.bfloat16)
    gate_grad = cotangent * branch
    grad_w_out = contract_rows(gated, branch_grad)
    gate_branch_grad = (gated_grad * mixed * silu_slope(gate_branch)).astype(jnp.bfloat16)

    wide_grad = jnp.zeros((tokens + 2 * RIM, inner), jnp.float32)
    x_proj, dt_proj, small = [], [], []
    conv_w_cols, conv_b_cols, dt_cols, skip_cols = [], [], [], []
    for d in range(2):
        conv_sum, active, rank_low, in_coef, out_coef, logit, step, masked, driven = saved[d]
        active_float = active.astype(jnp.float32)
        driven_grad = (dg0, dg1)[d]
        step_grad = (dec0, dec1)[d] + driven_grad * active_float
        active_grad = driven_grad * step + mixed_grad * d_skip[d][None, :]
        skip_cols.append(jnp.sum(mixed_grad * active_float, axis=0))
        logit_grad = step_grad * jax.nn.sigmoid(logit)
        dt_cols.append(jnp.sum(logit_grad, axis=0))
        logit_low = logit_grad.astype(jnp.bfloat16)
        dt_proj.append(contract_rows(logit_low, rank_low))
        rank_grad = contract_cols(logit_low, w_dt[d])
        proj_grad = jnp.concatenate([rank_grad, in_grads[d], out_grads[d]], axis=1).astype(
            jnp.bfloat16
        )
        x_proj.append(contract_rows(active, proj_grad))
        active_total = active_grad + contract_cols(proj_grad, w_x[d])
        conv_grad = active_total * silu_slope(conv_sum)
        conv_b_cols.append(jnp.sum(conv_grad, axis=0))
        for k in range(taps):
            offset = k - (taps - 1) if d == 0 else taps - 1 - k
            masked_grad = conv_grad * same(offset).astype(jnp.float32)[:, None]
            conv_w_cols.append(
                jnp.sum(
                    masked_grad * conv_wide[RIM + offset : RIM + offset + tokens], axis=0
                )
            )
            wide_grad = wide_grad + jnp.pad(
                conv_w[d, k][None, :] * masked_grad, ((RIM + offset, RIM - offset), (0, 0))
            )
    input_grad = wide_grad.astype(jnp.bfloat16)
    grad_in_conv = contract_rows(mixer_in, input_grad)
    grad_in_gate = contract_rows(mixer_in[own], gate_branch_grad)
    norm_wide = contract_cols(input_grad, w_in[:, :inner])
    norm_wide = norm_wide.at[own].add(contract_cols(gate_branch_grad, w_in[:, inner:]))

    mod_low = lax.dot_general(
        onehot,
        jnp.concatenate([norm_wide, norm_wide * normed], axis=1),
        (((0,), (0,)), ((), ())),
        precision=HIGHEST,
        preferred_element_type=jnp.float32,
    )
    mod_high = lax.dot_general(
        onehot[own],
        gate_grad,
        (((0,), (0,)), ((), ())),
        precision=HIGHEST,
        preferred_element_type=jnp.float32,
    )
    mod_part = jnp.concatenate([mod_low, mod_high], axis=1)
    mod_part = jnp.pad(mod_part, ((0, -seq_count % 8), (0, 0)))
    rim = jnp.concatenate([norm_wide[:RIM], norm_wide[-RIM:]], axis=0)

    rows = inner // count
    pad_rows = -rows % 16
    mrows = model // count
    both = jnp.stack(
        [grad_in_conv.reshape(count, mrows, inner), grad_in_gate.reshape(count, mrows, inner)],
        axis=1,
    ).reshape(count, 2 * mrows, inner)
    cols = jnp.concatenate(
        [
            x_proj[0],
            x_proj[1],
            dt_proj[0],
            dt_proj[1],
            jnp.stack(conv_w_cols + conv_b_cols + dt_cols + skip_cols, axis=1),
            rate_grad.reshape(2 * states, inner).T,
        ],
        axis=1,
    )
    cols = jnp.pad(cols, ((0, 0), (0, -cols.shape[1] % LANES)))
    pieces = [both, grad_w_out.reshape(count, rows, model), cols.reshape(count, rows, -1)]
    whole = jnp.concatenate([p.astype(jnp.bfloat16) for p in pieces], axis=2)
    whole = jnp.pad(whole, ((0, 0), (0, pad_rows), (0, 0)))
    width = whole.shape[2]
    split = width // LANES // 2 * LANES
    whole = whole.reshape(groups, 2, 2, 2, rows + pad_rows, width)
    part_a = whole[..., :split].transpose(3, 2, 1, 0, 4, 5)
    part_b = whole[..., split:].transpose(3, 1, 2, 0, 4, 5)
    part_a = part_a.reshape(2, 4 * groups, rows + pad_rows, split)
    part_b = part_b.reshape(2, 4 * groups, rows + pad_rows, width - split)
    share_a, share_b, mod_grad, edges = reduce_shares(part_a, part_b, mod_part, rim, count)
    share = jnp.concatenate([share_a, share_b], axis=1)[:rows]

    edges = jnp.concatenate(
        [
            jnp.where(me > 0, edges[:RIM], 0.0),
            jnp.zeros((tokens - 2 * RIM, model), jnp.float32),
            jnp.where(me < count - 1, edges[RIM:], 0.0),
        ],
        axis=0,
    )
    norm_grad = norm_wide[own] + edges
    scaled = norm_grad * (1.0 + scale_rows[own])
    normed_own = normed[own]
    grad_x = cotangent + rescale[own] * (
        scaled
        - jnp.mean(scaled, axis=1, keepdims=True)
        - normed_own * jnp.mean(scaled * normed_own, axis=1, keepdims=True)
    )

    my_cond = lax.dynamic_slice_in_dim(cond_act.astype(jnp.float32), me * mrows, mrows, axis=1)
    mod_grad = mod_grad[:seq_count]
    share_w_mod = lax.dot_general(
        my_cond,
        mod_grad,
        (((0,), (0,)), ((), ())),
        precision=HIGHEST,
        preferred_element_type=jnp.float32,
    )
    bias_cols = 3 * model // count
    share_b_mod = lax.dynamic_slice_in_dim(
        jnp.sum(mod_grad, axis=0), me * bias_cols, bias_cols, axis=0
    )

    w_in_share = jnp.concatenate([share[:mrows, :inner], share[mrows:, :inner]], axis=1)
    w_out_share = share[:, inner : inner + model]
    rest = share[:, inner + model :]
    proj = rank + 2 * states
    at = 0

    def take(number):
        nonlocal at
        piece = rest[:, at : at + number]
        at += number
        return piece

    share_w_x = jnp.stack([take(proj), take(proj)])
    share_w_dt = jnp.stack([take(rank).T, take(rank).T])
    share_conv_w = take(2 * taps).T.reshape(2, taps, rows)
    share_conv_b = take(2).T
    share_dt_bias = take(2).T
    share_skip = take(2).T
    share_a_log = take(2 * states).T.reshape(2, states, rows)
    return (
        output,
        grad_x,
        share_w_mod,
        share_b_mod,
        w_in_share,
        share_conv_w,
        share_conv_b,
        share_w_x,
        share_w_dt,
        share_dt_bias,
        share_a_log,
        share_skip,
        w_out_share,
    )


def solution(mesh):
    in_specs = (P("seq", None),) + (P(),) * 13 + (P("seq", None),)
    out_specs = (
        P("seq", None),
        P("seq", None),
        P("seq", None),
        P("seq"),
        P("seq", None),
        P(None, None, "seq"),
        P(None, "seq"),
        P(None, "seq", None),
        P(None, None, "seq"),
        P(None, "seq"),
        P(None, None, "seq"),
        P(None, "seq"),
        P("seq", None),
    )
    return jax.shard_map(
        functools.partial(on_device, mesh.shape["seq"]),
        mesh=mesh,
        in_specs=in_specs,
        out_specs=out_specs,
        check_vma=False,
    )
```

profile of v0, /device:TPU:0, one launch (start us, length us, event | category | flops | bytes accessed | tf_op | source)
XLA Modules:
  0.0 266.7 jit_solution(15637285583172259910)
XLA Ops:
  0.7 1.5 fusion.89
  2.1 2.3 collective-permute-start
  18.6 1.4 multiply_reduce_fusion.8
  21.4 2.3 fusion.6
  24.5 4.3 %fusion.25 = (bf16[1536]{0:T(1024)(128)(2,1)}, bf16[1536]{0:T(1024)(128)(2,1)}, f32[128,1536]{1,0:T(8,128)}, bf16[128,1536]{1,0:T(8,128)(2,1)S(1)}, f32[128,1536...) fusion(f32[128,1536]{1,0:T(8,128)S(1)} %fusion.6, ...), kind=kOutput, calls=%fused_computation.53 | convolution fusion | flops 310735872 | bytes 13263872 | tf_op jit(solution)/shard_map/dot_general | solution.py:39
  32.3 1.5 multiply_convert_fusion.5
  33.8 2.3 convert_multiply_fusion.3
  36.1 3.2 %convert_multiply_fusion.7 = (f32[128,1536]{1,0:T(8,128)S(1)}, f32[128,1536]{1,0:T(8,128)S(1)}, f32[128,1536]{1,0:T(8,128)}) fusion(bf16[128,1536]{1,0:T(8,128)(2,1)} %copy-done.27, pred[128]{0:T(512)(128)(4,1)} %get-tuple-element.192, f32[1536]{0:T(1024)} %get-tuple-element.119, bf16[2,48,1536]{2,1,0:T(8,128)(2,1)} %param.26, f32[128,80]{0,1:T(8,128)S(1)} %fusion.37), kind=kOutput, calls=%fused_computation.37 | convolution fusion | flops 20840448 | bytes 2920960 | tf_op jit(solution)/shard_map/dot_general | solution.py:659
  39.7 1.5 broadcast_in_dim.36.in1
  43.8 10.9 %summaries.1 = f32[2,12,3,16,128]{4,3,2,1,0:T(8,128)S(1)} custom-call(f32[128,1536]{1,0:T(8,128)S(1)} %get-tuple-element.151.step0, f32[128,1536]{1,0:T(8,128)S(1)} %get-tuple-element.149.step1, f32[128,1536]{1,0:T(8,128)S(1)} %get-tuple-element.150.drv0, f32[128,1536]{1,0:T(8,128)S(1)} %get-tuple-element.148.drv1, f32[128,1536]{1,0:T(8,128)S(1)} %copy-done.7, ...), custom_call_target="tpu_custom_call" | custom-call | tf_op jit(solution)/shard_map/summaries/pallas_call | solution.py:95
  54.7 27.6 %carries.1 = f32[24,2,16,128]{3,2,1,0:T(8,128)S(1)} custom-call(f32[8,3,3,16,128]{4,3,2,1,0:T(8,128)S(1)} %bitcast.110), custom_call_target="tpu_custom_call" | custom-call | tf_op jit(solution)/shard_map/carries/pallas_call | solution.py:218
  85.5 38.3 %scans.1 = (f32[128,1536]{1,0:T(8,128)S(1)}, f32[128,1536]{1,0:T(8,128)S(1)}, f32[128,1536]{1,0:T(8,128)S(1)}, f32[128,1536]{1,0:T(8,128)S(1)}, f32[128,1536]{1,...) custom-call(f32[128,1536]{1,0:T(8,128)} %copy-done.6, ...), custom_call_target="tpu_custom_call" | custom-call | tf_op jit(solution)/shard_map/scans/pallas_call | solution.py:368
  123.9 4.3 %fusion.82 = (bf16[1536]{0:T(1024)(128)(2,1)}, bf16[128,1536]{1,0:T(8,128)(2,1)S(1)}, bf16[128,1536]{1,0:T(8,128)(2,1)}, f32[128,1536]{1,0:T(8,128)}, bf16[1536]{0:T(1024)(128)(2,1)}, /*index=5*/bf16[128,1536]{1,0:T(8,128)(2,1)S(1)}) fusion(f32[128,1536]{1,0:T(8,128)S(1)} %copy-done.41, f32[128,1536]{1,0:T(8,128)S(1)} %get-tuple-element.41, ...), kind=kLoop, calls=%fused_computation.216 | loop fusion | flops 6484992 | bytes 10635264 | tf_op jit(solution)/shard_map/reduce_sum | solution.py:717
  134.3 2.5 broadcast_multiply_fusion.1
  139.1 1.8 multiply_reduce_fusion
  142.7 2.3 convolution_convert_fusion.2
  146.5 1.8 convolution_convert_fusion
  148.3 2.2 convolution_convert_fusion.1
  152.3 1.7 fusion.76
  155.3 4.2 %concatenate.46 = bf16[1536,302]{0,1:T(8,128)(2,1)S(1)} concatenate(bf16[1536,80]{0,1:T(8,128)(2,1)} %convolution_convert_fusion.5, bf16[1536,80]{0,1:T(8,128)(2,1)} %convolution_convert_fusion.4, bf16[1536,48]{0,1:T(8,128)(2,1)} %convolution_convert_fusion.7, bf16[1536,48]{0,1:T(8,128)(2,1)} %convolution_convert_fusion.6, bf16[1536,1]{0,1:T(2,128)(2,1)S(1)} %stack.91, ...), dimensions={1} | concatenate | bytes 1855488 | tf_op jit(solution)/shard_map/concatenate | solution.py:770
  159.5 1.4 copy.89
  160.9 2.8 %pad_maximum_fusion = bf16[32,2,24,1536]{3,2,1,0:T(8,128)(2,1)S(1)} fusion(bf16[32,1,24,1536]{3,2,1,0:T(8,128)(2,1)} %bitcast.117, bf16[32,1,24,1536]{3,2,1,0:T(8,128)(2,1)} %bitcast.116), kind=kLoop, calls=%fused_computation | loop fusion | flops 2359296 | bytes 9437184 | tf_op jit(solution)/shard_map/stack | solution.py:766
  165.6 2.4 copy.82
  169.4 71.4 %reduce_shares.1 = (f32[48,1280]{1,0:T(8,128)S(1)}, f32[48,1408]{1,0:T(8,128)S(1)}, f32[8,2304]{1,0:T(8,128)S(1)}, f32[16,768]{1,0:T(8,128)S(1)}) custom-call(bf16[2,16,48,1280]{3,2,1,0:T(8,128)(2,1)S(1)} %bitcast.109, bf16[2,16,48,1408]{3,2,1,0:T(8,128)(2,1)} %bitcast.114, f32[8,2304]{1,0:T(8,128)S(1)} %select_maximum_fusion.mod, ...), custom_call_target="tpu_custom_call" | custom-call | tf_op jit(solution)/shard_map/reduce_shares/pallas_call | solution.py:548
  249.3 2.4 fusion.77
  252.2 1.7 fusion.58
  254.0 1.4 copy.85
  258.1 1.4 copy.84
  259.5 1.4 copy.83
  260.9 1.4 pad_maximum_fusion.8
  262.3 1.7 pad_maximum_fusion.3
  264.6 2.1 convert_add_fusion
  (358 shorter events, 54.8 us)
Async XLA Ops:
  0.6 10.1 %copy-start = (bf16[768,2304]{1,0:T(8,128)(2,1)S(1)}, bf16[768,2304]{1,0:T(8,128)(2,1)}, u32[]{:S(2)}) copy-start(bf16[768,2304]{1,0:T(8,128)(2,1)} %param.20) | copy-start | bytes 10616836
  2.1 15.2 %collective-permute-start = (bf16[8,768]{1,0:T(8,128)(2,1)}, bf16[8,768]{1,0:T(8,128)(2,1)S(1)}, u32[]{:S(2)}, u32[]{:S(2)}) collective-permute-start(bf16[8,768]{1,0:T(8,128)(2,1)} %get-tuple-element.169), channel_id=1, source_target_pairs={{0,1},{1,2},{2,3},{3,4},{4,5},{5,6},{6,7},{7,8},{8,9},{9,10},{10,1... | collective-permute-start | bytes 36872 | tf_op jit(solution)/shard_map/ppermute | solution.py:605
  4.5 12.8 %collective-permute-start.1 = (bf16[8,768]{1,0:T(8,128)(2,1)}, bf16[8,768]{1,0:T(8,128)(2,1)}, u32[]{:S(2)}, u32[]{:S(2)}) collective-permute-start(bf16[8,768]{1,0:T(8,128)(2,1)} %get-tuple-element.170), channel_id=1, source_target_pairs={{1,0},{2,1},{3,2},{4,3},{5,4},{6,5},{7,6},{8,7},{9,8},{10,9},{11,1... | collective-permute-start | bytes 36872 | tf_op jit(solution)/shard_map/ppermute | solution.py:606
  7.7 8.0 %copy-start.120 = (s32[128]{0:T(128)S(1)}, s32[128]{0:T(128)}, u32[]{:S(2)}) copy-start(s32[128]{0:T(128)} %and_select_fusion) | copy-start | bytes 1540
  7.7 8.0 %copy-start.90 = (f32[2,1536]{1,0:T(2,128)S(1)}, f32[2,1536]{1,0:T(2,128)}, u32[]{:S(2)}) copy-start(f32[2,1536]{1,0:T(2,128)} %param.29) | copy-start | bytes 36868
  12.8 11.5 %copy-start.23 = (f32[144,2304]{1,0:T(8,128)}, f32[144,2304]{1,0:T(8,128)S(1)}, u32[]{:S(2)}) copy-start(f32[144,2304]{1,0:T(8,128)S(1)} %fusion.61) | copy-start | bytes 3981316
  13.7 15.1 %copy-start.78 = (f32[1536]{0:T(1024)}, f32[1536]{0:T(1024)S(1)}, u32[]{:S(2)}) copy-start(f32[1536]{0:T(1024)S(1)} %get-tuple-element.111) | copy-start | bytes 18436
  13.7 15.1 %copy-start.80 = (f32[1536]{0:T(1024)}, f32[1536]{0:T(1024)S(1)}, u32[]{:S(2)}) copy-start(f32[1536]{0:T(1024)S(1)} %get-tuple-element.112) | copy-start | bytes 18436
  13.7 15.1 %copy-start.82 = (f32[1536]{0:T(1024)}, f32[1536]{0:T(1024)S(1)}, u32[]{:S(2)}) copy-start(f32[1536]{0:T(1024)S(1)} %get-tuple-element.113) | copy-start | bytes 18436
  13.7 15.1 %copy-start.94 = (f32[1536]{0:T(1024)}, f32[1536]{0:T(1024)S(1)}, u32[]{:S(2)}) copy-start(f32[1536]{0:T(1024)S(1)} %get-tuple-element.108) | copy-start | bytes 18436
  24.4 9.3 %copy-start.49 = (bf16[2,48,1536]{2,1,0:T(8,128)(2,1)S(1)}, bf16[2,48,1536]{2,1,0:T(8,128)(2,1)}, u32[]{:S(2)}) copy-start(bf16[2,48,1536]{2,1,0:T(8,128)(2,1)} %param.26) | copy-start | bytes 884740
  36.1 7.7 %copy-start.3 = (f32[128,1536]{1,0:T(8,128)}, f32[128,1536]{1,0:T(8,128)S(1)}, u32[]{:S(2)}) copy-start(f32[128,1536]{1,0:T(8,128)S(1)} %get-tuple-element.148.drv1) | copy-start | bytes 2359300
  36.1 7.7 %copy-start.4 = (f32[128,1536]{1,0:T(8,128)}, f32[128,1536]{1,0:T(8,128)S(1)}, u32[]{:S(2)}) copy-start(f32[128,1536]{1,0:T(8,128)S(1)} %get-tuple-element.149.step1) | copy-start | bytes 2359300
  36.1 7.7 %copy-start.7 = (f32[128,1536]{1,0:T(8,128)S(1)}, f32[128,1536]{1,0:T(8,128)}, u32[]{:S(2)}) copy-start(f32[128,1536]{1,0:T(8,128)} %get-tuple-element.125.seed) | copy-start | bytes 2359300
  36.1 7.7 %copy-start.9 = (f32[2,16,1536]{2,1,0:T(8,128)S(1)}, f32[2,16,1536]{2,1,0:T(8,128)}, u32[]{:S(2)}) copy-start(f32[2,16,1536]{2,1,0:T(8,128)} %negate_multiply_fusion.rate) | copy-start | bytes 589828
  39.3 15.4 %copy-start.5 = (f32[128,1536]{1,0:T(8,128)}, f32[128,1536]{1,0:T(8,128)S(1)}, u32[]{:S(2)}) copy-start(f32[128,1536]{1,0:T(8,128)S(1)} %get-tuple-element.150.drv0) | copy-start | bytes 2359300
  39.3 15.4 %copy-start.6 = (f32[128,1536]{1,0:T(8,128)}, f32[128,1536]{1,0:T(8,128)S(1)}, u32[]{:S(2)}) copy-start(f32[128,1536]{1,0:T(8,128)S(1)} %get-tuple-element.151.step0) | copy-start | bytes 2359300
  39.7 15.0 %copy-start.2 = (f32[128,16,128]{2,1,0:T(8,128)}, f32[128,16,128]{2,1,0:T(8,128)S(1)}, u32[]{:S(2)}) copy-start(f32[128,16,128]{2,1,0:T(8,128)S(1)} %broadcast_in_dim.35.in0) | copy-start | bytes 3145732
  43.8 40.4 %copy-start.59 = (bf16[128,16,16]{0,2,1:T(8,128)(2,1)S(1)}, bf16[128,16,16]{0,2,1:T(8,128)(2,1)}, u32[]{:S(2)}) copy-start(bf16[128,16,16]{0,2,1:T(8,128)(2,1)} %get-tuple-element.184) | copy-start | bytes 196612
  43.8 40.5 %copy-start.58 = (bf16[128,16,16]{0,2,1:T(8,128)(2,1)S(1)}, bf16[128,16,16]{0,2,1:T(8,128)(2,1)}, u32[]{:S(2)}) copy-start(bf16[128,16,16]{0,2,1:T(8,128)(2,1)} %get-tuple-element.183) | copy-start | bytes 196612
  85.4 38.4 %copy-start.25 = (bf16[128,1536]{1,0:T(8,128)(2,1)S(1)}, bf16[128,1536]{1,0:T(8,128)(2,1)}, u32[]{:S(2)}) copy-start(bf16[128,1536]{1,0:T(8,128)(2,1)} %copy-done.24) | copy-start | bytes 1179652
  85.4 38.4 %copy-start.28 = (bf16[128,1536]{1,0:T(8,128)(2,1)S(1)}, bf16[128,1536]{1,0:T(8,128)(2,1)}, u32[]{:S(2)}) copy-start(bf16[128,1536]{1,0:T(8,128)(2,1)} %copy-done.27) | copy-start | bytes 1179652
  85.4 38.4 %copy-start.36 = (f32[128,1536]{1,0:T(8,128)S(1)}, f32[128,1536]{1,0:T(8,128)}, u32[]{:S(2)}) copy-start(f32[128,1536]{1,0:T(8,128)} %copy-done.35) | copy-start | bytes 2359300
  85.4 38.4 %copy-start.38 = (f32[128,1536]{1,0:T(8,128)S(1)}, f32[128,1536]{1,0:T(8,128)}, u32[]{:S(2)}) copy-start(f32[128,1536]{1,0:T(8,128)} %get-tuple-element.195) | copy-start | bytes 2359300
  85.4 38.4 %copy-start.41 = (f32[128,1536]{1,0:T(8,128)S(1)}, f32[128,1536]{1,0:T(8,128)}, u32[]{:S(2)}) copy-start(f32[128,1536]{1,0:T(8,128)} %get-tuple-element.194) | copy-start | bytes 2359300
  85.4 38.4 %copy-start.52 = (f32[128,1536]{1,0:T(8,128)S(1)}, f32[128,1536]{1,0:T(8,128)}, u32[]{:S(2)}) copy-start(f32[128,1536]{1,0:T(8,128)} %get-tuple-element.193) | copy-start | bytes 2359300
  85.4 38.4 %copy-start.75 = (f32[1536]{0:T(1024)S(1)}, f32[1536]{0:T(1024)}, u32[]{:S(2)}) copy-start(f32[1536]{0:T(1024)} %get-tuple-element.117) | copy-start | bytes 18436
  85.5 38.4 %copy-start.77 = (f32[1536]{0:T(1024)S(1)}, f32[1536]{0:T(1024)}, u32[]{:S(2)}) copy-start(f32[1536]{0:T(1024)} %get-tuple-element.116) | copy-start | bytes 18436
  123.9 9.3 %copy-start.67 = (f32[128,16]{0,1:T(8,128)S(1)}, f32[128,16]{0,1:T(8,128)}, u32[]{:S(2)}) copy-start(f32[128,16]{0,1:T(8,128)} %copy-done.66) | copy-start | bytes 24580
  169.4 72.2 %copy-start.93 = (f32[144]{0:T(256)S(1)}, f32[144]{0:T(256)}, u32[]{:S(2)}) copy-start(f32[144]{0:T(256)} %copy-done.91) | copy-start | bytes 1732
  169.4 79.9 %copy-start.119 = (f32[128]{0:T(128)S(1)}, f32[128]{0:T(128)}, u32[]{:S(2)}) copy-start(f32[128]{0:T(128)} %pad.59.clone) | copy-start | bytes 1540
  245.7 21.1 %copy-start.1 = (bf16[768,2304]{1,0:T(8,128)(2,1)S(1)}, bf16[768,2304]{1,0:T(8,128)(2,1)}, u32[]{:S(2)}) copy-start(bf16[768,2304]{1,0:T(8,128)(2,1)} %param.20) | copy-start | bytes 10616836
  (94 other events, 349.2 us)
where the time goes:
time: 268 us; the launch traced here: 267 us
  Pallas kernels  148 us (55%)
  local copies, waits for them, and re-layouts  43.8 us (16%)
  matrix products  35.9 us (13%)
  other arithmetic  32.8 us (12%)
  starting transfers between devices  3.64 us (1%)
    pallas_call x1, Pallas kernels, reduce_shares(): pl.pallas_call(functools.partial(reduce_kernel, count), in_specs=[vmem] *...  71.4 us
    pallas_call x1, Pallas kernels, scans(): pl.pallas_call(scan_kernel, grid=(width // cols,), in_specs=[rows] * 5 +...  38.3 us
    pallas_call x1, Pallas kernels, carries(): pl.pallas_call(functools.partial(carry_kernel, count), in_specs=[vmem], o...  27.6 us
    pallas_call x1, Pallas kernels, summaries(): pl.pallas_call(summary_kernel, grid=(width // cols,), in_specs=[rows] * 5...  10.9 us
    dot_general x7, matrix products, contract_cols(): lax.dot_general(left, right, (((1,), (1,)), ((), ())), preferred_element_...  10.8 us
    dot_general x7, matrix products, contract_rows(): lax.dot_general(left, right, (((0,), (0,)), ((), ())), preferred_element_...  9.82 us
    unnamed x254, local copies, waits for them, and re-layouts  9.35 us
    dot_general x2, matrix products, on_device(): jnp.dot(rank_low, w_dt[d], preferred_element_type=jnp.float32)  5.51 us
  transfers between devices with their start and end apart: 2, of which 0 were waited for; matrix products, arithmetic and copies ran while one was open for 4% of the time, Pallas kernels for 0%

commit v1 on v0

v1 whole, which is shorter than its diff:
```python
import functools

import jax
import jax.numpy as jnp
from jax import lax
from jax.experimental import pallas as pl
from jax.experimental.pallas import tpu as pltpu
from jax.sharding import PartitionSpec as P

EPSILON = 1e-06
HIGHEST = lax.Precision.HIGHEST
MESH = pl.DeviceIdType.MESH
LANES = 128
LOG2E = 1.4426950408889634
LN2 = 0.6931471805599453
CUT_STEP = 1e9
PLANE = 8
RIM = 8
CHUNK = 16
COLS = 256
MIB = 1024 * 1024
F32 = jnp.float32
BF16 = jnp.bfloat16
VMEM = pl.BlockSpec(memory_space=pltpu.VMEM)
ANY = pl.BlockSpec(memory_space=pl.ANY)


def shaped(shape, dtype=F32):
    return jax.ShapeDtypeStruct(shape, dtype)


def dot(left, right, dims=((1,), (0,)), precision=None):
    return lax.dot_general(
        left, right, (dims, ((), ())), precision=precision, preferred_element_type=F32
    )


def contract_rows(left, right, precision=None):
    return dot(left, right, ((0,), (0,)), precision)


def contract_cols(left, right):
    return dot(left, right, ((1,), (1,)))


def sigmoid(values):
    return 1.0 / (1.0 + jnp.exp(-values))


def silu_slope(values):
    sigma = sigmoid(values)
    return sigma * (1.0 + values * (1.0 - sigma))


def softplus(values):
    return jnp.maximum(values, 0.0) + jnp.log1p(jnp.exp(-jnp.abs(values)))


def tile_at(start):
    return pl.ds(pl.multiple_of(start, LANES), LANES)


def row_of(ref, first, j, lanes):
    eight = pl.ds(pl.multiple_of(first + j // 8 * 8, 8), 8)
    return ref.at[eight, lanes][j % 8 : j % 8 + 1, :]


def segments(positions, bounds):
    total = jnp.full(positions.shape, -1, jnp.int32)
    for bound in bounds:
        total = total + (positions >= bound).astype(jnp.int32)
    return total


def read_bounds(lengths):
    bounds = [jnp.int32(0)]
    for j in range(lengths.shape[0]):
        bounds.append(bounds[-1] + lengths[j])
    return bounds


def rows_iota(rows):
    return lax.broadcasted_iota(jnp.int32, (rows, LANES), 0)


def offset_of(d, k, taps):
    return k - (taps - 1) if d == 0 else taps - 1 - k


def head_kernel(
    lengths,
    hidden,
    below,
    above,
    condition,
    b_mod,
    conv_w,
    conv_b,
    dt_bias,
    a_log,
    grad_out,
    w_mod_any,
    w_in_any,
    w_x_any,
    w_dt_any,
    w_out_any,
    mixer,
    mixer_own,
    normed,
    rescale,
    scale1,
    gate_rows,
    branch_grad,
    conv_keep,
    gate_branch,
    gated_grad,
    seed,
    conv_sum,
    active,
    rank_low,
    logit,
    masked,
    driven,
    in_spread,
    out_spread,
    in_blk,
    out_blk,
    rate,
    rate_tiles,
    sums,
    masks,
    hot,
    w_mod,
    w_conv,
    w_gate,
    w_x,
    w_dt,
    w_out,
    conv_wide,
    proj,
    modulation,
    sems,
):
    tokens, model = hidden.shape
    inner = seed.shape[1]
    rank = w_dt.shape[1]
    states = a_log.shape[1]
    taps = conv_w.shape[1]
    wide = tokens + 2 * RIM
    tiles = inner // LANES

    loads = [
        pltpu.make_async_copy(src, dst, sems.at[i])
        for i, (src, dst) in enumerate(
            (
                (w_mod_any, w_mod),
                (w_in_any.at[:, pl.ds(0, inner)], w_conv),
                (w_in_any.at[:, pl.ds(inner, inner)], w_gate),
                (w_out_any, w_out),
                (w_x_any, w_x),
                (w_dt_any, w_dt),
            )
        )
    ]
    for load in loads:
        load.start()

    first = lax.axis_index("seq") * tokens
    bounds = read_bounds(lengths)
    position = first + rows_iota(tokens)
    segment = segments(position, bounds)
    for offset in range(1 - taps, taps):
        masks[offset + taps - 1] = (segments(position + offset, bounds) == segment).astype(F32)
    wide_segment = segments(first - RIM + rows_iota(wide), bounds)
    lane = lax.broadcasted_iota(jnp.int32, (wide, LANES), 1)
    hot[...] = (wide_segment == lane).astype(F32)

    rate[...] = -jnp.exp(a_log[...]) * LOG2E
    for d in range(2):
        for c in range(tiles):
            rate_tiles[d * tiles + c] = rate[d, :, c * LANES : (c + 1) * LANES]

    x = jnp.concatenate(
        [below[...].astype(F32), hidden[...].astype(F32), above[...].astype(F32)], axis=0
    )
    centered = x - jnp.mean(x, axis=1, keepdims=True)
    scaling = lax.rsqrt(jnp.mean(centered * centered, axis=1, keepdims=True) + EPSILON)
    normal = centered * scaling
    normed[...] = normal
    rescale[...] = jnp.broadcast_to(scaling[RIM : RIM + tokens], (tokens, LANES))

    cond = condition[...]
    cond_act = (cond * sigmoid(cond)).astype(BF16)
    loads[0].wait()
    seqs = condition.shape[0]
    modulation[0:seqs, :] = dot(cond_act, w_mod[...]) + b_mod[...]
    for c in range(model // LANES):
        lanes = slice(c * LANES, (c + 1) * LANES)

        def rows_for(part, segs):
            total = jnp.zeros(segs.shape, F32)
            for j in range(seqs):
                at = part * model + c * LANES
                total = jnp.where(segs == j, modulation[j : j + 1, at : at + LANES], total)
            return total

        one_scale = 1.0 + rows_for(1, wide_segment)
        mixed_in = normed[:, lanes] * one_scale + rows_for(0, wide_segment)
        mixer[:, lanes] = mixed_in.astype(BF16)
        mixer_own[:, lanes] = mixed_in[RIM : RIM + tokens].astype(BF16)
        scale1[:, lanes] = one_scale[RIM : RIM + tokens]
        gate = rows_for(2, segment)
        gate_rows[:, lanes] = gate
        branch_grad[:, lanes] = (grad_out[:, lanes].astype(F32) * gate).astype(BF16)

    for load in loads[1:]:
        load.wait()

    proj[...] = jnp.zeros_like(proj)

    def block(b, none):
        cols = pl.ds(pl.multiple_of(b * COLS, COLS), COLS)
        conv = dot(mixer[...], w_conv[:, cols]).astype(BF16)
        conv_keep[:, cols] = conv
        conv_wide[...] = conv.astype(F32)
        gate = dot(mixer_own[...], w_gate[:, cols])
        gate_branch[:, cols] = gate
        back = contract_cols(branch_grad[...], w_out[cols, :])
        gated_grad[:, cols] = back
        seed[:, cols] = back * (gate * sigmoid(gate))
        for d in range(2):
            acts = []
            for c in range(COLS // LANES):
                lanes = tile_at(b * COLS + c * LANES)
                here = slice(c * LANES, (c + 1) * LANES)
                total = jnp.broadcast_to(conv_b[d : d + 1, lanes], (tokens, LANES))
                for k in range(taps):
                    offset = offset_of(d, k, taps)
                    total = total + conv_w[d, k : k + 1, lanes] * (
                        conv_wide[RIM + offset : RIM + offset + tokens, here]
                        * masks[offset + taps - 1]
                    )
                conv_sum[d, :, lanes] = total
                act = (total * sigmoid(total)).astype(BF16)
                active[d, :, lanes] = act
                acts.append(act)
            proj[d] += dot(jnp.concatenate(acts, axis=1), w_x[d, cols, :])
        return none

    lax.fori_loop(0, inner // COLS, block, 0)

    place = lax.rem(lax.broadcasted_iota(jnp.int32, (tokens, CHUNK * states), 0), CHUNK)
    owner = lax.broadcasted_iota(jnp.int32, (tokens, CHUNK * states), 1) // states
    on_diag = place == owner
    column = lax.rem(lax.broadcasted_iota(jnp.int32, (states, CHUNK * states), 1), states)
    repeat = (column == lax.broadcasted_iota(jnp.int32, (states, CHUNK * states), 0)).astype(BF16)
    for d in range(2):
        whole = proj[d]
        rank_low[d] = whole[:, :rank].astype(BF16)
        flipped = whole.T
        for start, blk, spread in (
            (rank, in_blk, in_spread),
            (rank + states, out_blk, out_spread),
        ):
            coef = whole[:, start : start + states].astype(BF16)
            blk[d] = jnp.where(on_diag, dot(coef, repeat), 0.0).astype(BF16)
            rows = flipped[start : start + states, :]
            for t in range(tokens):
                spread[d, t] = jnp.broadcast_to(rows[:, t : t + 1], (states, LANES))

    def stepping(b, none):
        cols = pl.ds(pl.multiple_of(b * COLS, COLS), COLS)
        for d in range(2):
            value = dot(rank_low[d], w_dt[d, :, cols]) + dt_bias[d : d + 1, cols]
            step = softplus(value)
            keep = masks[taps - 2] if d == 0 else masks[taps]
            keep = jnp.concatenate([keep] * (COLS // LANES), axis=1)
            logit[d, :, cols] = value
            masked[d, :, cols] = jnp.where(keep > 0.5, step, CUT_STEP)
            driven[d, :, cols] = step * active[d, :, cols].astype(F32)
        return none

    lax.fori_loop(0, inner // COLS, stepping, 0)

    per = COLS // LANES

    def summary(b, none):
        lanes = [tile_at(b * COLS + c * LANES) for c in range(per)]

        def group(i, carry):
            carry = list(carry)
            for k in range(8):
                for d in range(2):
                    start = pl.multiple_of((i if d == 0 else tokens // 8 - 1 - i) * 8, 8)
                    j = k if d == 0 else 7 - k
                    in_row = in_spread[d, start + j]
                    out_row = out_spread[d, start + j]
                    for c in range(per):
                        state, decay, adj = carry[d * per + c]
                        now = jnp.exp2(
                            row_of(masked.at[d], start, j, lanes[c]) * rate[d, :, lanes[c]]
                        )
                        state = now * state + in_row * row_of(driven.at[d], start, j, lanes[c])
                        decay = decay * now
                        adj = adj + decay * (out_row * row_of(seed, start, j, lanes[c]))
                        carry[d * per + c] = (state, decay, adj)
            return tuple(carry)

        zero = jnp.zeros((states, LANES), F32)
        one = jnp.ones((states, LANES), F32)
        carry = lax.fori_loop(
            0, tokens // 8, group, tuple((zero, one, zero) for _ in range(2 * per))
        )
        for d in range(2):
            for c in range(per):
                state, decay, adj = carry[d * per + c]
                down, up = (adj, state) if d == 0 else (state, adj)
                at = d * tiles + b * per + c
                sums[at, 0] = down.astype(BF16)
                sums[at, 1] = three_pieces(
                    jnp.sum(masked[d, :, lanes[c]], axis=0, keepdims=True), states
                )
                sums[at, 2] = up.astype(BF16)
        return none

    lax.fori_loop(0, inner // COLS, summary, 0)


def three_pieces(row, states):
    high = row.astype(BF16).astype(F32)
    middle = (row - high).astype(BF16).astype(F32)
    lowest = row - high - middle
    at = lax.broadcasted_iota(jnp.int32, (states, row.shape[-1]), 0)
    return jnp.where(
        at == 0, high, jnp.where(at == 1, middle, jnp.where(at == 2, lowest, 0.0))
    ).astype(BF16)


def head(lengths, hidden, below, above, condition, b_mod, conv_w, conv_b, dt_bias, a_log, grad_out, weights):
    w_mod, w_in, w_x, w_dt, w_out = weights
    tokens, model = hidden.shape
    inner = w_in.shape[1] // 2
    rank = w_dt.shape[1]
    states = a_log.shape[1]
    taps = conv_w.shape[1]
    wide = tokens + 2 * RIM
    both = (2, tokens, inner)
    spread = (2, tokens, states, LANES)
    diag = (2, tokens, CHUNK * states)
    outs = dict(
        mixer=shaped((wide, model), BF16),
        mixer_own=shaped((tokens, model), BF16),
        normed=shaped((wide, model)),
        rescale=shaped((tokens, LANES)),
        scale1=shaped((tokens, model)),
        gate_rows=shaped((tokens, model)),
        branch_grad=shaped((tokens, model), BF16),
        conv_keep=shaped((wide, inner), BF16),
        gate_branch=shaped((tokens, inner)),
        gated_grad=shaped((tokens, inner)),
        seed=shaped((tokens, inner)),
        conv_sum=shaped(both),
        active=shaped(both, BF16),
        rank_low=shaped((2, tokens, rank), BF16),
        logit=shaped(both),
        masked=shaped(both),
        driven=shaped(both),
        in_spread=shaped(spread),
        out_spread=shaped(spread),
        in_blk=shaped(diag, BF16),
        out_blk=shaped(diag, BF16),
        rate=shaped(a_log.shape),
        rate_tiles=shaped((2 * inner // LANES, states, LANES)),
        sums=shaped((2 * inner // LANES, 3, states, LANES), BF16),
        masks=shaped((2 * taps - 1, tokens, LANES)),
        hot=shaped((wide, LANES)),
    )
    results = pl.pallas_call(
        head_kernel,
        in_specs=[pl.BlockSpec(memory_space=pltpu.SMEM)] + [VMEM] * 10 + [ANY] * 5,
        out_specs=[VMEM] * len(outs),
        out_shape=list(outs.values()),
        scratch_shapes=[
            pltpu.VMEM(w_mod.shape, BF16),
            pltpu.VMEM((model, inner), BF16),
            pltpu.VMEM((model, inner), BF16),
            pltpu.VMEM(w_x.shape, BF16),
            pltpu.VMEM(w_dt.shape, BF16),
            pltpu.VMEM(w_out.shape, BF16),
            pltpu.VMEM((wide, COLS), F32),
            pltpu.VMEM((2, tokens, w_x.shape[2]), F32),
            pltpu.VMEM((8, w_mod.shape[1]), F32),
            pltpu.SemaphoreType.DMA((6,)),
        ],
        compiler_params=pltpu.CompilerParams(vmem_limit_bytes=56 * MIB),
        name="head",
    )(
        lengths,
        hidden,
        below,
        above,
        condition,
        b_mod.reshape(1, -1),
        conv_w,
        conv_b,
        dt_bias,
        a_log,
        grad_out,
        w_mod,
        w_in,
        w_x,
        w_dt,
        w_out,
    )
    return dict(zip(outs, results))


def carry_kernel(
    count, sums, rate, entering, got, total, others, back, send1, recv1, send2, recv2, send3, recv3
):
    groups = count // PLANE
    me = lax.axis_index("seq")
    mine = lax.rem(me, PLANE)
    level = me // PLANE
    base = level * PLANE
    share, _, states, _ = sums.shape
    share = share // PLANE
    here = pl.ds(mine * share, share)

    barrier = pltpu.get_barrier_semaphore()
    for k in range(1, PLANE):
        pl.semaphore_signal(
            barrier, inc=1, device_id=(base + lax.rem(mine + k, PLANE),), device_id_type=MESH
        )
    for k in range(1, groups):
        pl.semaphore_signal(
            barrier,
            inc=1,
            device_id=(lax.rem(level + k, groups) * PLANE + mine,),
            device_id_type=MESH,
        )
    pl.semaphore_wait(barrier, PLANE - 1 + groups - 1)

    first = []
    for k in range(1, PLANE):
        peer = lax.rem(mine + k, PLANE)
        copy = pltpu.make_async_remote_copy(
            src_ref=sums.at[pl.ds(peer * share, share)],
            dst_ref=got.at[mine],
            send_sem=send1.at[k],
            recv_sem=recv1.at[k],
            device_id=(base + peer,),
            device_id_type=MESH,
        )
        copy.start()
        first.append(copy)
    got[mine] = sums[here]
    others[level] = jnp.zeros(others.shape[1:], BF16)
    for copy in first:
        copy.wait_recv()

    block = (share, states, LANES)
    rates = rate[here]

    def whole(pieces):
        pieces = pieces.astype(F32)
        return pieces[:, 0:1] + pieces[:, 1:2] + pieces[:, 2:3]

    times = [whole(got[j, :, 1]) for j in range(PLANE)]
    decays = [jnp.exp2(rates * time) for time in times]
    up = jnp.zeros(block, F32)
    down = jnp.zeros(block, F32)
    time = times[0]
    for j in range(PLANE):
        up = decays[j] * up + got[j, :, 2].astype(F32)
        if j:
            time = time + times[j]
    for j in reversed(range(PLANE)):
        down = decays[j] * down + got[j, :, 0].astype(F32)
    total[0] = down.astype(BF16)
    for c in range(share):
        total[1, c] = three_pieces(time[c], states)
    total[2] = up.astype(BF16)

    second = []
    for k in range(1, groups):
        other = lax.rem(level + k, groups)
        start = jnp.where(other > level, 1, 0)
        copy = pltpu.make_async_remote_copy(
            src_ref=total.at[pl.ds(start, 2)],
            dst_ref=others.at[level],
            send_sem=send2.at[k],
            recv_sem=recv2.at[k],
            device_id=(other * PLANE + mine,),
            device_id_type=MESH,
        )
        copy.start()
        second.append(copy)
    for copy in second:
        copy.wait_recv()

    up = jnp.zeros(block, F32)
    for g in range(groups):
        decay = jnp.exp2(rates * whole(others[g, 0]))
        up = jnp.where(g < level, decay * up + others[g, 1].astype(F32), up)
    down = jnp.zeros(block, F32)
    for g in reversed(range(groups)):
        decay = jnp.exp2(rates * whole(others[g, 1]))
        down = jnp.where(g > level, decay * down + others[g, 0].astype(F32), down)
    for j in range(PLANE):
        back[j, :, 0] = up.astype(BF16)
        up = decays[j] * up + got[j, :, 2].astype(F32)
    for j in reversed(range(PLANE)):
        back[j, :, 1] = down.astype(BF16)
        down = decays[j] * down + got[j, :, 0].astype(F32)

    third = []
    for k in range(1, PLANE):
        peer = lax.rem(mine + k, PLANE)
        copy = pltpu.make_async_remote_copy(
            src_ref=back.at[peer],
            dst_ref=entering.at[here],
            send_sem=send3.at[k],
            recv_sem=recv3.at[k],
            device_id=(base + peer,),
            device_id_type=MESH,
        )
        copy.start()
        third.append(copy)
    entering[here] = back[mine]
    for copy in third:
        copy.wait_recv()
    for copy in first + second + third:
        copy.wait_send()


def carries(sums, rate, count):
    rows, _, states, _ = sums.shape
    share = rows // PLANE
    groups = count // PLANE
    entering = pl.pallas_call(
        functools.partial(carry_kernel, count),
        in_specs=[VMEM, VMEM],
        out_specs=VMEM,
        out_shape=shaped((rows, 2, states, LANES), BF16),
        scratch_shapes=[
            pltpu.VMEM((PLANE, share, 3, states, LANES), BF16),
            pltpu.VMEM((3, share, states, LANES), BF16),
            pltpu.VMEM((groups, 2, share, states, LANES), BF16),
            pltpu.VMEM((PLANE, share, 2, states, LANES), BF16),
            pltpu.SemaphoreType.DMA((PLANE,)),
            pltpu.SemaphoreType.DMA((PLANE,)),
            pltpu.SemaphoreType.DMA((groups,)),
            pltpu.SemaphoreType.DMA((groups,)),
            pltpu.SemaphoreType.DMA((PLANE,)),
            pltpu.SemaphoreType.DMA((PLANE,)),
        ],
        compiler_params=pltpu.CompilerParams(
            collective_id=0, has_side_effects=True, vmem_limit_bytes=32 * MIB
        ),
        name="carries",
    )(sums, rate)
    return entering.reshape(2, rows // 2, 2, states, LANES)


def states_kernel(masked, driven, seed, in_spread, out_blk, rate, entering, mixed, out_grad, kept):
    tokens, cols = seed.shape
    per = cols // LANES
    states = rate.shape[1]
    chunks = tokens // CHUNK

    @pl.when(pl.program_id(0) == 0)
    def _():
        out_grad[...] = jnp.zeros_like(out_grad)

    mixed[...] = jnp.zeros_like(mixed)
    for c in range(per):
        lanes = pl.ds(c * LANES, LANES)
        kept[0, 0:states, lanes] = entering[0, c, 0]
        kept[1, tokens * states : (tokens + 1) * states, lanes] = entering[1, c, 1]

    def forward(i, carry):
        carry = list(carry)
        for d in range(2):
            first = pl.multiple_of((i if d == 0 else chunks - 1 - i) * CHUNK, CHUNK)
            slot = pl.multiple_of((first + 1 - d) * states, states)
            block = kept.at[d, pl.ds(slot, CHUNK * states), :]
            for k in range(CHUNK):
                j = k if d == 0 else CHUNK - 1 - k
                in_row = in_spread[d, first + j]
                for c in range(per):
                    lanes = pl.ds(c * LANES, LANES)
                    now = jnp.exp2(row_of(masked.at[d], first, j, lanes) * rate[d, :, lanes])
                    state = now * carry[d * per + c] + in_row * row_of(
                        driven.at[d], first, j, lanes
                    )
                    block[j * states : (j + 1) * states, lanes] = state.astype(BF16)
                    carry[d * per + c] = state
            here = pl.ds(first, CHUNK)
            mixed[here, :] += dot(out_blk[d, here, :], block[...])
            out_grad[d, here, :] += contract_cols(seed[here, :].astype(BF16), block[...])
        return tuple(carry)

    start = tuple(entering[d, c, d].astype(F32) for d in range(2) for c in range(per))
    lax.fori_loop(0, chunks, forward, start)


def block_specs(tokens, states):
    wide = CHUNK * states
    return dict(
        both=pl.BlockSpec((2, tokens, COLS), lambda b: (0, 0, b)),
        rows=pl.BlockSpec((tokens, COLS), lambda b: (0, b)),
        spread=pl.BlockSpec((2, tokens, states, LANES), lambda b: (0, 0, 0, 0)),
        diag=pl.BlockSpec((2, tokens, wide), lambda b: (0, 0, 0)),
        rate=pl.BlockSpec((2, states, COLS), lambda b: (0, 0, b)),
        entering=pl.BlockSpec((2, COLS // LANES, 2, states, LANES), lambda b: (0, b, 0, 0, 0)),
        kept=pl.BlockSpec((2, (tokens + 1) * states, COLS), lambda b: (0, 0, b)),
    )


def run_states(h, entering):
    tokens, inner = h["seed"].shape
    states = h["rate"].shape[1]
    s = block_specs(tokens, states)
    return pl.pallas_call(
        states_kernel,
        grid=(inner // COLS,),
        in_specs=[s["both"], s["both"], s["rows"], s["spread"], s["diag"], s["rate"], s["entering"]],
        out_specs=[s["rows"], s["diag"], s["kept"]],
        out_shape=[
            shaped((tokens, inner)),
            shaped((2, tokens, CHUNK * states)),
            shaped((2, (tokens + 1) * states, inner), BF16),
        ],
        compiler_params=pltpu.CompilerParams(vmem_limit_bytes=48 * MIB),
        name="states",
    )(h["masked"], h["driven"], h["seed"], h["in_spread"], h["out_blk"], h["rate"], entering)


def adjoints_kernel(
    masked,
    driven,
    seed,
    out_spread,
    in_blk,
    rate,
    entering,
    kept,
    decay_grad,
    driven_grad,
    in_grad,
    rate_grad,
    rows_a,
    rows_b,
    rows_c,
    rows_d,
):
    tokens, cols = seed.shape
    per = cols // LANES
    states = rate.shape[1]
    chunks = tokens // CHUNK
    wide = CHUNK * states
    ones = (
        lax.broadcasted_iota(jnp.int32, (CHUNK, wide), 1) // states
        == lax.broadcasted_iota(jnp.int32, (CHUNK, wide), 0)
    ).astype(BF16)

    @pl.when(pl.program_id(0) == 0)
    def _():
        in_grad[...] = jnp.zeros_like(in_grad)

    def backward(i, carry):
        carry = list(carry)
        for d in range(2):
            first = pl.multiple_of((chunks - 1 - i if d == 0 else i) * CHUNK, CHUNK)
            slot = pl.multiple_of((first + d) * states, states)
            before = kept.at[d, pl.ds(slot, wide), :]
            adjs = (rows_a, rows_b)[d]
            slopes = (rows_c, rows_d)[d]
            for k in range(CHUNK):
                j = CHUNK - 1 - k if d == 0 else k
                out_row = out_spread[d, first + j]
                part = slice(j * states, (j + 1) * states)
                for c in range(per):
                    lanes = pl.ds(c * LANES, LANES)
                    coming, total = carry[d * per + c]
                    step = row_of(masked.at[d], first, j, lanes)
                    now = jnp.exp2(step * rate[d, :, lanes])
                    adj = out_row * row_of(seed, first, j, lanes) + coming
                    coming = now * adj
                    slope = coming * before[part, lanes].astype(F32) * rate[d, :, lanes]
                    total = total + slope * step
                    adjs[part, lanes] = adj.astype(BF16)
                    slopes[part, lanes] = slope.astype(BF16)
                    carry[d * per + c] = (coming, total)
            here = pl.ds(first, CHUNK)
            driven_grad[d, here, :] = dot(in_blk[d, here, :], adjs[...])
            in_grad[d, here, :] += contract_cols(driven[d, here, :].astype(BF16), adjs[...])
            decay_grad[d, here, :] = dot(ones, slopes[...]) * LN2
        return tuple(carry)

    zero = jnp.zeros((states, LANES), F32)
    start = tuple((entering[d, c, 1 - d].astype(F32), zero) for d in range(2) for c in range(per))
    carry = lax.fori_loop(0, chunks, backward, start)
    for d in range(2):
        for c in range(per):
            rate_grad[d, :, c * LANES : (c + 1) * LANES] = carry[d * per + c][1] * LN2


def run_adjoints(h, entering, kept):
    tokens, inner = h["seed"].shape
    states = h["rate"].shape[1]
    s = block_specs(tokens, states)
    return pl.pallas_call(
        adjoints_kernel,
        grid=(inner // COLS,),
        in_specs=[
            s["both"],
            s["both"],
            s["rows"],
            s["spread"],
            s["diag"],
            s["rate"],
            s["entering"],
            s["kept"],
        ],
        out_specs=[s["both"], s["both"], s["diag"], s["rate"]],
        out_shape=[
            shaped((2, tokens, inner)),
            shaped((2, tokens, inner)),
            shaped((2, tokens, CHUNK * states)),
            shaped((2, states, inner)),
        ],
        scratch_shapes=[pltpu.VMEM((CHUNK * states, COLS), BF16)] * 4,
        compiler_params=pltpu.CompilerParams(vmem_limit_bytes=48 * MIB),
        name="adjoints",
    )(
        h["masked"],
        h["driven"],
        h["seed"],
        h["out_spread"],
        h["in_blk"],
        h["rate"],
        entering,
        kept,
    )


def slot_of(o, count, order):
    bits = [o & 1, o >> 1 & 1, o >> 2 & 1]
    groups = count // PLANE
    later = (bits[1], bits[2]) if order == "xy" else (bits[2], bits[1])
    return bits[0], (later[0] * 2 + later[1]) * groups + o // PLANE


def slot_rows(count, inner):
    rows = inner // count
    return rows + -rows % 16


def stacked_rows(source, stage, o, rows):
    half = source.shape[1] // 2
    part = pl.ds(o * rows, rows)
    if rows % 8 == 0:
        return jnp.concatenate([source[part, :half], source[part, half:]], axis=0)
    stage[0:rows, :] = source[part, :half]
    stage[rows : 2 * rows, :] = source[part, half:]
    return stage[...]


def mid_kernel(
    count,
    states_sum,
    active,
    d_skip,
    gate_branch,
    gated_grad,
    gate_rows,
    branch_grad,
    mixer_own,
    hidden,
    grad_out,
    w_out,
    output,
    gate_grad,
    gate_branch_grad,
    slots_out,
    slots_gate,
    gated,
    branch,
    whole_out,
    whole_gate,
    stage,
):
    tokens, inner = states_sum.shape
    model = hidden.shape[1]
    branch[...] = jnp.zeros_like(branch)

    def block(b, none):
        cols = pl.ds(pl.multiple_of(b * COLS, COLS), COLS)
        mixed = states_sum[:, cols]
        for d in range(2):
            mixed = mixed + d_skip[d : d + 1, cols] * active[d, :, cols].astype(F32)
        gate = gate_branch[:, cols]
        sigma = sigmoid(gate)
        now = (mixed * (gate * sigma)).astype(BF16)
        gated[:, cols] = now
        slope = sigma * (1.0 + gate * (1.0 - sigma))
        back = (gated_grad[:, cols] * mixed * slope).astype(BF16)
        gate_branch_grad[:, cols] = back
        branch[...] += dot(now, w_out[cols, :])
        whole_out[cols, :] = contract_rows(now, branch_grad[...])
        whole_gate[:, cols] = contract_rows(mixer_own[...], back)
        return none

    lax.fori_loop(0, inner // COLS, block, 0)
    output[...] = (hidden[...].astype(F32) + gate_rows[...] * branch[...]).astype(BF16)
    gate_grad[...] = grad_out[...].astype(F32) * branch[...]
    rows, mrows = inner // count, model // count
    for o in range(count):
        first, rest = slot_of(o, count, "xy")
        slots_out[first, rest, 0:rows] = whole_out[o * rows : (o + 1) * rows, :].astype(BF16)
        first, rest = slot_of(o, count, "yx")
        slots_gate[first, rest] = stacked_rows(whole_gate, stage, o, mrows).astype(BF16)


def run_mid(h, count, states_sum, d_skip, hidden, grad_out, w_out):
    tokens, inner = states_sum.shape
    model = hidden.shape[1]
    slots = shaped((2, count // 2, slot_rows(count, inner), model), BF16)
    return pl.pallas_call(
        functools.partial(mid_kernel, count),
        in_specs=[VMEM] * 11,
        out_specs=[VMEM] * 5,
        out_shape=[
            shaped((tokens, model), BF16),
            shaped((tokens, model)),
            shaped((tokens, inner), BF16),
            slots,
            slots,
        ],
        scratch_shapes=[
            pltpu.VMEM((tokens, inner), BF16),
            pltpu.VMEM((tokens, model), F32),
            pltpu.VMEM((inner, model), F32),
            pltpu.VMEM((model, inner), F32),
            pltpu.VMEM((slot_rows(count, inner), model), F32),
        ],
        compiler_params=pltpu.CompilerParams(vmem_limit_bytes=56 * MIB),
        name="mid",
    )(
        states_sum,
        h["active"],
        d_skip,
        h["gate_branch"],
        h["gated_grad"],
        h["gate_rows"],
        h["branch_grad"],
        h["mixer_own"],
        hidden,
        grad_out,
        w_out,
    )


def post_kernel(
    count,
    decay_grad,
    driven_grad,
    in_acc,
    out_acc,
    rate_grad,
    logit,
    active,
    rank_low,
    seed,
    conv_sum,
    conv_keep,
    masks,
    hot,
    d_skip,
    conv_w,
    mixer,
    normed,
    gate_grad,
    gate_branch_grad,
    w_x,
    w_dt,
    w_in,
    norm_wide,
    mod_part,
    slots_a,
    slots_b,
    active_grad,
    rank_grad,
    proj_grad,
    conv_wide,
    input_wide,
    whole_conv,
    whole_cols,
    small,
    stage,
):
    tokens, inner = seed.shape
    model = normed.shape[1]
    wide = normed.shape[0]
    taps = conv_w.shape[1]
    rank = w_dt.shape[1]
    proj = w_x.shape[2]
    states = rate_grad.shape[1]
    seqs = mod_part.shape[0]
    rank_grad[...] = jnp.zeros_like(rank_grad)
    small[...] = jnp.zeros_like(small)
    at_conv, at_bias, at_dt, at_skip, at_rate = (
        0,
        2 * taps,
        2 * taps + 2,
        2 * taps + 4,
        2 * taps + 8,
    )

    def column_sum(values):
        return jnp.sum(values, axis=0, keepdims=True)

    def through_steps(b, none):
        cols = pl.ds(pl.multiple_of(b * COLS, COLS), COLS)
        for d in range(2):
            act = active[d, :, cols].astype(F32)
            value = logit[d, :, cols]
            back = driven_grad[d, :, cols]
            grown = seed[:, cols]
            grad = (decay_grad[d, :, cols] + back * act) * sigmoid(value)
            low = grad.astype(BF16)
            active_grad[d, :, cols] = back * softplus(value) + grown * d_skip[d : d + 1, cols]
            small[at_dt + d : at_dt + d + 1, cols] = column_sum(grad)
            small[at_skip + d : at_skip + d + 1, cols] = column_sum(grown * act)
            small[at_rate + d * states : at_rate + (d + 1) * states, cols] = rate_grad[d, :, cols]
            rank_grad[d] += contract_cols(low, w_dt[d, :, cols])
            start = 2 * proj + d * rank
            whole_cols[cols, start : start + rank] = contract_rows(low, rank_low[d])
        return none

    lax.fori_loop(0, inner // COLS, through_steps, 0)

    place = lax.rem(lax.broadcasted_iota(jnp.int32, (tokens, CHUNK * states), 0), CHUNK)
    owner = lax.broadcasted_iota(jnp.int32, (tokens, CHUNK * states), 1) // states
    on_diag = place == owner
    column = lax.rem(lax.broadcasted_iota(jnp.int32, (CHUNK * states, states), 0), states)
    gather = (column == lax.broadcasted_iota(jnp.int32, (CHUNK * states, states), 1)).astype(BF16)
    for d in range(2):
        proj_grad[d, :, 0:rank] = rank_grad[d].astype(BF16)
        for start, acc in ((rank, in_acc), (rank + states, out_acc)):
            kept = jnp.where(on_diag, acc[d], 0.0).astype(BF16)
            proj_grad[d, :, start : start + states] = dot(kept, gather).astype(BF16)

    norm_wide[...] = jnp.zeros_like(norm_wide)

    def through_conv(b, none):
        cols = pl.ds(pl.multiple_of(b * COLS, COLS), COLS)
        conv_wide[...] = conv_keep[:, cols].astype(F32)
        input_wide[...] = jnp.zeros_like(input_wide)
        for d in range(2):
            low = proj_grad[d]
            start = d * proj
            whole_cols[cols, start : start + proj] = contract_rows(active[d, :, cols], low)
            total = active_grad[d, :, cols] + contract_cols(low, w_x[d, cols, :])
            for c in range(COLS // LANES):
                lanes = tile_at(b * COLS + c * LANES)
                here = slice(c * LANES, (c + 1) * LANES)
                grad = total[:, here] * silu_slope(conv_sum[d, :, lanes])
                small[at_bias + d : at_bias + d + 1, lanes] = column_sum(grad)
                for k in range(taps):
                    offset = offset_of(d, k, taps)
                    window = slice(RIM + offset, RIM + offset + tokens)
                    part = grad * masks[offset + taps - 1]
                    at = at_conv + d * taps + k
                    small[at : at + 1, lanes] = column_sum(part * conv_wide[window, here])
                    input_wide[window, here] += conv_w[d, k : k + 1, lanes] * part
        low = input_wide[...].astype(BF16)
        whole_conv[:, cols] = contract_rows(mixer[...], low)
        norm_wide[...] += contract_cols(low, w_in[:, cols])
        gate_cols = pl.ds(pl.multiple_of(inner + b * COLS, COLS), COLS)
        norm_wide[RIM : RIM + tokens, :] += contract_cols(
            gate_branch_grad[:, cols], w_in[:, gate_cols]
        )
        whole_cols[cols, 2 * (proj + rank) :] = small[:, cols].T
        return none

    lax.fori_loop(0, inner // COLS, through_conv, 0)

    seq_rows = hot[:, 0:seqs]
    grads = norm_wide[...]
    mod_part[:, 0:model] = contract_rows(seq_rows, grads, HIGHEST)
    mod_part[:, model : 2 * model] = contract_rows(seq_rows, grads * normed[...], HIGHEST)
    mod_part[:, 2 * model :] = contract_rows(
        hot[RIM : RIM + tokens, 0:seqs], gate_grad[...], HIGHEST
    )

    rows, mrows = inner // count, model // count
    cut = slots_a.shape[3]
    rest = model - cut
    for o in range(count):
        both = stacked_rows(whole_conv, stage, o, mrows).astype(BF16)
        first, later = slot_of(o, count, "xy")
        slots_a[first, later] = both[:, :cut]
        first, later = slot_of(o, count, "yx")
        slots_b[first, later, :, 0:rest] = both[:, cut:]
        slots_b[first, later, 0:rows, rest:] = whole_cols[o * rows : (o + 1) * rows, :].astype(BF16)


def column_width(proj, rank, taps, states):
    small = 2 * taps + 8 + 2 * states
    small = small + -small % 8
    total = 2 * (proj + rank) + small
    return small + -total % LANES, total + -total % LANES


def run_post(h, count, adjoint_side, out_acc, mid_side, d_skip, conv_w, w_x, w_dt, w_in):
    decay_grad, driven_grad, in_acc, rate_grad = adjoint_side
    gate_grad, gate_branch_grad = mid_side
    tokens, inner = h["seed"].shape
    wide, model = h["normed"].shape
    rank = w_dt.shape[1]
    proj = w_x.shape[2]
    states = rate_grad.shape[1]
    small, width = column_width(proj, rank, conv_w.shape[1], states)
    rows = slot_rows(count, inner)
    cut = (model + width) // 2 // LANES * LANES
    return pl.pallas_call(
        functools.partial(post_kernel, count),
        in_specs=[VMEM] * 22,
        out_specs=[VMEM] * 4,
        out_shape=[
            shaped((wide, model)),
            shaped((8, 3 * model)),
            shaped((2, count // 2, rows, cut), BF16),
            shaped((2, count // 2, rows, model + width - cut), BF16),
        ],
        scratch_shapes=[
            pltpu.VMEM((2, tokens, inner), F32),
            pltpu.VMEM((2, tokens, rank), F32),
            pltpu.VMEM((2, tokens, proj), BF16),
            pltpu.VMEM((wide, COLS), F32),
            pltpu.VMEM((wide, COLS), F32),
            pltpu.VMEM((model, inner), F32),
            pltpu.VMEM((inner, width), F32),
            pltpu.VMEM((small, inner), F32),
            pltpu.VMEM((rows, model), F32),
        ],
        compiler_params=pltpu.CompilerParams(vmem_limit_bytes=58 * MIB),
        name="post",
    )(
        decay_grad,
        driven_grad,
        in_acc,
        out_acc,
        rate_grad,
        h["logit"],
        h["active"],
        h["rank_low"],
        h["seed"],
        h["conv_sum"],
        h["conv_keep"],
        h["masks"],
        h["hot"],
        d_skip,
        conv_w,
        h["mixer"],
        h["normed"],
        gate_grad,
        gate_branch_grad,
        w_x,
        w_dt,
        w_in,
    )


def reduce_kernel(count, orders, *refs):
    number = len(orders)
    refs = list(refs)

    def take(size):
        taken = refs[:size]
        del refs[:size]
        return taken

    parts, (mod, rim) = take(number), take(2)
    shares, (out_mod, out_rim) = take(number), take(2)
    got1, got2, got3, got4 = take(number), take(number), take(number), take(number)
    m1, m2, m3, m4 = take(4)
    send, recv, send_far, recv_far = take(4)
    groups = count // PLANE
    me = lax.axis_index("seq")
    bits = [lax.rem(me, 2), lax.rem(me // 2, 2), lax.rem(me // 4, 2)]
    flips = [me + (1 - 2 * bits[i]) * (1 << i) for i in range(3)]
    level = me // PLANE
    low = lax.rem(me, PLANE)
    left = lax.rem(me + count - 1, count)
    right = lax.rem(me + 1, count)
    far = [lax.rem(level + k, groups) for k in range(1, groups)]

    barrier = pltpu.get_barrier_semaphore()
    peers = flips + [left, right] + [g * PLANE + low for g in far]
    for peer in peers:
        pl.semaphore_signal(barrier, inc=1, device_id=(peer,), device_id_type=MESH)
    pl.semaphore_wait(barrier, len(peers))

    started = []

    def push(src, dst, sems, slot, peer):
        copy = pltpu.make_async_remote_copy(
            src_ref=src,
            dst_ref=dst,
            send_sem=sems[0].at[slot],
            recv_sem=sems[1].at[slot],
            device_id=(peer,),
            device_id_type=MESH,
        )
        copy.start()
        started.append(copy)
        return copy

    near_sems, far_sems = (send, recv), (send_far, recv_far)

    def near(src, dst, slot, peer):
        return push(src, dst, near_sems, slot, peer)

    def add(into, own, first):
        def one(i, none):
            into[i] = (into[i].astype(F32) + own[first + i].astype(F32)).astype(BF16)
            return none

        lax.fori_loop(0, into.shape[0], one, 0)

    edges = [
        near(rim.at[pl.ds(0, RIM)], out_rim.at[pl.ds(RIM, RIM)], 0, left),
        near(rim.at[pl.ds(rim.shape[0] - RIM, RIM)], out_rim.at[pl.ds(0, RIM)], 1, right),
    ]
    base = 5
    mods = near(mod, m1, 2, flips[0])
    waits = [
        near(parts[p].at[1 - bits[0]], got1[p], base + p, flips[0]) for p in range(number)
    ]
    half = 2 * groups
    mods.wait_recv()
    m1[...] += mod[...]
    mods = near(m1, m2, 3, flips[1])
    for p, order in enumerate(orders):
        i = 1 if order == "xy" else 2
        waits[p].wait_recv()
        add(got1[p], parts[p].at[bits[0]], 0)
        waits[p] = near(
            got1[p].at[pl.ds((1 - bits[i]) * half, half)], got2[p], base + number + p, flips[i]
        )
    mods.wait_recv()
    m2[...] += m1[...]
    mods = near(m2, m3, 4, flips[2])
    for p, order in enumerate(orders):
        i, j = (1, 2) if order == "xy" else (2, 1)
        waits[p].wait_recv()
        add(got2[p], got1[p], bits[i] * half)
        waits[p] = near(
            got2[p].at[pl.ds((1 - bits[j]) * groups, groups)],
            got3[p],
            base + 2 * number + p,
            flips[j],
        )
    mods.wait_recv()
    m3[...] += m2[...]
    last = []
    for k, g in enumerate(far):
        last.append(push(m3, m4.at[level], far_sems, k, g * PLANE + low))
    m4[level] = m3[...]
    for p, order in enumerate(orders):
        j = 2 if order == "xy" else 1
        waits[p].wait_recv()
        add(got3[p], got2[p], bits[j] * groups)
        for k, g in enumerate(far):
            slot = (p + 1) * len(far) + k
            last.append(push(got3[p].at[g], got4[p].at[level], far_sems, slot, g * PLANE + low))
        got4[p][level] = got3[p][level]
    for copy in last + edges:
        copy.wait_recv()
    for into, held in list(zip(shares, got4)) + [(out_mod, m4)]:
        total = held[0].astype(F32)
        for g in range(1, groups):
            total = total + held[g].astype(F32)
        into[...] = total
    for copy in started:
        copy.wait_send()


def reduce_shares(parts, orders, mod, rim, count):
    groups = count // PLANE
    number = len(parts)
    shapes = [part.shape[-2:] for part in parts]

    def slots(size):
        return [pltpu.VMEM((size,) + shape, BF16) for shape in shapes]

    near = 5 + 3 * number
    far = (number + 1) * (groups - 1)
    return pl.pallas_call(
        functools.partial(reduce_kernel, count, orders),
        in_specs=[VMEM] * (number + 2),
        out_specs=[VMEM] * (number + 2),
        out_shape=[shaped(shape) for shape in shapes]
        + [shaped(mod.shape), shaped((2 * RIM, rim.shape[1]))],
        scratch_shapes=slots(4 * groups)
        + slots(2 * groups)
        + slots(groups)
        + slots(groups)
        + [pltpu.VMEM(mod.shape, F32)] * 3
        + [pltpu.VMEM((groups,) + mod.shape, F32)]
        + [pltpu.SemaphoreType.DMA((near,))] * 2
        + [pltpu.SemaphoreType.DMA((far,))] * 2,
        compiler_params=pltpu.CompilerParams(
            collective_id=1, has_side_effects=True, vmem_limit_bytes=48 * MIB
        ),
        name="reduce_shares",
    )(*parts, mod, rim)


def finish_kernel(
    count,
    proj,
    rank,
    taps,
    states,
    share_out,
    share_gate,
    share_a,
    share_b,
    mod,
    edges,
    my_cond,
    norm_wide,
    normed,
    rescale,
    scale1,
    grad_out,
    grad_x,
    w_mod,
    b_mod,
    w_in,
    conv_w,
    conv_b,
    w_x,
    w_dt,
    dt_bias,
    a_log,
    d_skip,
    w_out,
):
    me = lax.axis_index("seq")
    tokens, model = grad_out.shape
    mrows, double = w_in.shape
    inner = double // 2
    rows = w_out.shape[0]
    seqs = my_cond.shape[0]
    cut = share_a.shape[1]

    w_out[...] = share_out[0:rows, :]
    w_in[:, 0:cut] = share_a[0:mrows, :]
    w_in[:, cut:model] = share_b[0:mrows, 0 : model - cut]
    w_in[:, model : model + cut] = share_a[mrows : 2 * mrows, :]
    w_in[:, model + cut : inner] = share_b[mrows : 2 * mrows, 0 : model - cut]
    w_in[:, inner : inner + model] = share_gate[0:mrows, :]
    w_in[:, inner + model :] = share_gate[mrows : 2 * mrows, :]

    start = model - cut
    for d in range(2):
        w_x[d] = share_b[0:rows, start + d * proj : start + (d + 1) * proj]
    start = start + 2 * proj
    flipped = share_b[:, model - cut :].T
    at = 2 * proj
    for d in range(2):
        w_dt[d] = flipped[at + d * rank : at + (d + 1) * rank, 0:rows]
    at = at + 2 * rank
    for d in range(2):
        conv_w[d] = flipped[at + d * taps : at + (d + 1) * taps, 0:rows]
    at = at + 2 * taps
    conv_b[...] = flipped[at : at + 2, 0:rows]
    dt_bias[...] = flipped[at + 2 : at + 4, 0:rows]
    d_skip[...] = flipped[at + 4 : at + 6, 0:rows]
    at = at + 8
    for d in range(2):
        a_log[d] = flipped[at + d * states : at + (d + 1) * states, 0:rows]

    cond = my_cond[...]
    cond_act = (cond * sigmoid(cond)).astype(BF16).astype(F32)
    totals = mod[0:seqs, :]
    w_mod[...] = contract_rows(cond_act, totals, HIGHEST)
    b_mod[...] = jnp.sum(totals, axis=0, keepdims=True)

    norm_grad = norm_wide[RIM : RIM + tokens, :]
    low = jnp.where(me > 0, edges[0:RIM, :], 0.0)
    high = jnp.where(me < count - 1, edges[RIM:, :], 0.0)
    middle = jnp.zeros((tokens - 2 * RIM, model), F32)
    norm_grad = norm_grad + jnp.concatenate([low, middle, high], axis=0)
    scaled = norm_grad * scale1[...]
    normal = normed[RIM : RIM + tokens, :]
    grad_x[...] = grad_out[...].astype(F32) + rescale[:, 0:1] * (
        scaled
        - jnp.mean(scaled, axis=1, keepdims=True)
        - normal * jnp.mean(scaled * normal, axis=1, keepdims=True)
    )


def on_device(
    count,
    hidden,
    condition,
    seq_lengths,
    w_mod,
    b_mod,
    w_in,
    conv_w,
    conv_b,
    w_x,
    w_dt,
    dt_bias,
    a_log,
    d_skip,
    w_out,
    grad_out,
):
    tokens, model = hidden.shape
    inner = w_in.shape[1] // 2
    rank = w_dt.shape[1]
    proj = w_x.shape[2]
    states = a_log.shape[1]
    taps = conv_w.shape[1]
    seqs = condition.shape[0]
    me = lax.axis_index("seq")
    rows, mrows = inner // count, model // count

    below = lax.ppermute(hidden[-RIM:], "seq", [(i, i + 1) for i in range(count - 1)])
    above = lax.ppermute(hidden[:RIM], "seq", [(i + 1, i) for i in range(count - 1)])
    h = head(
        seq_lengths,
        hidden,
        below,
        above,
        condition,
        b_mod,
        conv_w,
        conv_b,
        dt_bias,
        a_log,
        grad_out,
        (w_mod, w_in, w_x, w_dt, w_out),
    )
    entering = carries(h["sums"], h["rate_tiles"], count)
    states_sum, out_acc, kept = run_states(h, entering)
    output, gate_grad, gate_branch_grad, slots_out, slots_gate = run_mid(
        h, count, states_sum, d_skip, hidden, grad_out, w_out
    )
    adjoint_side = run_adjoints(h, entering, kept)
    norm_wide, mod_part, slots_a, slots_b = run_post(
        h, count, adjoint_side, out_acc, (gate_grad, gate_branch_grad), d_skip, conv_w, w_x, w_dt, w_in
    )
    share_out, share_gate, share_a, share_b, mod, edges = reduce_shares(
        (slots_out, slots_gate, slots_a, slots_b), ("xy", "yx", "xy", "yx"), mod_part, norm_wide, count
    )
    my_cond = lax.dynamic_slice_in_dim(condition, me * mrows, mrows, axis=1)
    results = pl.pallas_call(
        functools.partial(finish_kernel, count, proj, rank, taps, states),
        in_specs=[VMEM] * 12,
        out_specs=[VMEM] * 12,
        out_shape=[
            shaped((tokens, model)),
            shaped((mrows, 3 * model)),
            shaped((1, 3 * model)),
            shaped((mrows, 2 * inner)),
            shaped((2, taps, rows)),
            shaped((2, rows)),
            shaped((2, rows, proj)),
            shaped((2, rank, rows)),
            shaped((2, rows)),
            shaped((2, states, rows)),
            shaped((2, rows)),
            shaped((rows, model)),
        ],
        compiler_params=pltpu.CompilerParams(vmem_limit_bytes=32 * MIB),
        name="finish",
    )(
        share_out,
        share_gate,
        share_a,
        share_b,
        mod,
        edges,
        my_cond,
        norm_wide,
        h["normed"],
        h["rescale"],
        h["scale1"],
        grad_out,
    )
    bias_cols = 3 * model // count
    share_b_mod = lax.dynamic_slice_in_dim(results[2][0], me * bias_cols, bias_cols, axis=0)
    return (output,) + tuple(results[:2]) + (share_b_mod,) + tuple(results[3:])


def solution(mesh):
    in_specs = (P("seq", None),) + (P(),) * 13 + (P("seq", None),)
    out_specs = (
        P("seq", None),
        P("seq", None),
        P("seq", None),
        P("seq"),
        P("seq", None),
        P(None, None, "seq"),
        P(None, "seq"),
        P(None, "seq", None),
        P(None, None, "seq"),
        P(None, "seq"),
        P(None, None, "seq"),
        P(None, "seq"),
        P("seq", None),
    )
    return jax.shard_map(
        functools.partial(on_device, mesh.shape["seq"]),
        mesh=mesh,
        in_specs=in_specs,
        out_specs=out_specs,
        check_vma=False,
    )
```

time: 268 us -> 219 us (0.82)
  Pallas kernels: 148 us -> 189 us
  matrix products: 35.9 us -> 0 us
  other arithmetic: 32.8 us -> 0 us
  local copies, waits for them, and re-layouts: 43.8 us -> 24 us
    pallas_call x4 -> x8, Pallas kernels: 148 us -> 189 us  [the longest x1 66.5 us: reduce_shares(): pl.pallas_call(functools.partial(reduce_kernel, count, orders), in_specs=...]
    dot_general x26 -> x0, matrix products: 35.9 us -> none  [the longest x7 10.8 us: contract_cols(): lax.dot_general(left, right, (((1,), (1,)), ((), ())), preferred_element_...]
    unnamed x254 -> x51, local copies, waits for them, and re-layouts: 9.35 us -> 20.6 us
    reduce_sum x8 -> x0, other arithmetic: 11.3 us -> none  [the longest x1 4.25 us: on_device(): dt_cols.append(jnp.sum(logit_grad, axis=0))]
    slice x17 -> x1, local copies, waits for them, and re-layouts: 10.1 us -> 0.73 us  [on_device(): hidden[:RIM]]
    transpose x8 -> x0, local copies, waits for them, and re-layouts: 7.91 us -> none  [the longest x1 2.42 us: on_device(): part_b = whole[..., split:].transpose(3, 1, 2, 0, 4, 5)]
    convert_element_type x8 -> x0, other arithmetic: 6 us -> none  [the longest x1 1.45 us: block_diag(): return wide.reshape(tokens, CHUNK * states).astype(jnp.bfloat16)]
    concatenate x3 -> x0, local copies, waits for them, and re-layouts: 6 us -> none  [the longest x1 4.22 us: on_device(): jnp.concatenate([x_proj[0], x_proj[1], dt_proj[0], dt_proj[1], jnp.stack(...]
  transfers between devices with their start and end apart: 2 -> 2, of which waited for: 0 -> 0; matrix products, arithmetic and copies ran while one was open for 4% -> 2% of each run, Pallas kernels for 0% -> 0%
where the time goes in v1:
time: 219 us; the launch traced here: 218 us
  Pallas kernels  189 us (86%)
  local copies, waits for them, and re-layouts  24 us (11%)
  starting transfers between devices  3.64 us (2%)
    pallas_call x1, Pallas kernels, reduce_shares(): pl.pallas_call(functools.partial(reduce_kernel, count, orders), in_specs=...  66.5 us
    pallas_call x1, Pallas kernels, head(): pl.pallas_call(head_kernel, in_specs=[pl.BlockSpec(memory_space=pltpu.SME...  29.6 us
    pallas_call x1, Pallas kernels, run_adjoints(): pl.pallas_call(adjoints_kernel, grid=(inner // COLS,), in_specs=[s['both'...  22.2 us
    pallas_call x1, Pallas kernels, run_states(): pl.pallas_call(states_kernel, grid=(inner // COLS,), in_specs=[s['both'],...  21.8 us
    pallas_call x1, Pallas kernels, carries(): pl.pallas_call(functools.partial(carry_kernel, count), in_specs=[VMEM, VM...  21 us
    unnamed x51, local copies, waits for them, and re-layouts  20.6 us
    pallas_call x1, Pallas kernels, run_post(): pl.pallas_call(functools.partial(post_kernel, count), in_specs=[VMEM] * 2...  18.3 us
    pallas_call x1, Pallas kernels, run_mid(): pl.pallas_call(functools.partial(mid_kernel, count), in_specs=[VMEM] * 11...  8.41 us
  transfers between devices with their start and end apart: 2, of which 0 were waited for; matrix products, arithmetic and copies ran while one was open for 2% of the time, Pallas kernels for 0%

profile of v1, /device:TPU:0, one launch (start us, length us, event | category | flops | bytes accessed | tf_op | source)
XLA Modules:
  0.0 217.8 jit_solution(67658411586817956)
XLA Ops:
  0.6 0.7 fusion
  1.4 2.3 %collective-permute-start = (bf16[8,768]{1,0:T(8,128)(2,1)S(1)}, bf16[8,768]{1,0:T(8,128)(2,1)S(1)}, u32[]{:S(2)}, u32[]{:S(2)}) collective-permute-start(bf16[8,768]{1,0:T(8,128)(2,1)S(1)} %get-tuple-element.134), channel_id=1, source_target_pairs={{0,1},{1,2},{2,3},{3,4},{4,5},{5,6},{6,7},{7,8},{8,9},{9,10},{10,1... | collective-permute-start | bytes 36872 | tf_op jit(solution)/shard_map/ppermute | solution.py:1338
  3.7 1.3 collective-permute-start.1
  5.0 0.8 constant_dynamic-slice_fusion.my_cond
  5.8 2.2 %copy.28.w_x_any.w_x = bf16[2,1536,80]{2,1,0:T(8,128)(2,1)} copy(bf16[2,1536,80]{1,2,0:T(8,128)(2,1)} %param.23) | data formatting | bytes 983040 | tf_op args[8]
  8.0 1.3 reshape.33.b_mod
  9.3 0.6 copy-done.23
  9.9 0.6 copy-done.24
  10.5 29.6 %head.1 = (bf16[144,768]{1,0:T(8,128)(2,1)}, bf16[128,768]{1,0:T(8,128)(2,1)}, f32[144,768]{1,0:T(8,128)}, f32[128,128]{1,0:T(8,128)}, f32[128,768]{1,0:T(8,128)...) custom-call(s32[6]{0:T(128)} %lengths.1, ...), custom_call_target="tpu_custom_call" | custom-call | tf_op jit(solution)/shard_map/head/pallas_call | solution.py:378
  40.2 1.0 copy-done.14
  41.1 0.9 copy-done.18
  42.1 21.0 %carries.1 = bf16[24,2,16,128]{3,2,1,0:T(8,128)(2,1)S(1)} custom-call(bf16[24,3,16,128]{3,2,1,0:T(8,128)(2,1)S(1)} %copy-done.14, f32[24,16,128]{2,1,0:T(8,128)S(1)} %copy-done.18), custom_call_target="tpu_custom_call" | custom-call | tf_op jit(solution)/shard_map/carries/pallas_call | solution.py:541
  63.0 1.1 copy-done
  64.1 1.4 copy-done.1
  65.6 1.4 copy-done.2
  67.0 0.9 copy-done.10
  67.9 0.9 copy-done.20
  68.8 21.8 %states.1 = (f32[128,1536]{1,0:T(8,128)S(1)}, f32[2,128,256]{2,1,0:T(8,128)S(1)}, bf16[2,2064,1536]{2,1,0:T(8,128)(2,1)}) custom-call(f32[2,128,1536]{2,1,0:T(8,128)S(1)} %copy-done.1, f32[2,128,1536]{2,1,0:T(8,128)S(1)} %copy-done.2, f32[128,1536]{1,0:T(8,128)S(1)} %copy-done, f32[2,128,16,128]{3,2,1,0:T(8,128)} %get-tuple-element.76.in_spread, ...), custom_call_target="tpu_custom_call" | custom-call | tf_op jit(solution)/shard_map/states/pallas_call | solution.py:625
  90.6 0.9 copy-done.12
  91.5 22.2 %adjoints.1 = (f32[2,128,1536]{2,1,0:T(8,128)S(1)}, f32[2,128,1536]{2,1,0:T(8,128)S(1)}, f32[2,128,256]{2,1,0:T(8,128)S(1)}, f32[2,16,1536]{2,1,0:T(8,128)S(1)}) custom-call(f32[2,128,1536]{2,1,0:T(8,128)} %get-tuple-element.73.masked, f32[2,128,1536]{2,1,0:T(8,128)} %get-tuple-element.74.driven, f32[128,1536]{1,0:T(8,128)S(1)} %copy-done, ...), custom_call_target="tpu_custom_call" | custom-call | tf_op jit(solution)/shard_map/adjoints/pallas_call | solution.py:714
  113.7 1.2 copy-done.7
  115.0 1.2 copy-done.8
  116.2 0.7 copy-done.16
  116.9 0.7 copy-done.17
  117.5 8.4 %mid.1 = (bf16[128,768]{1,0:T(8,128)(2,1)}, f32[128,768]{1,0:T(8,128)}, bf16[128,1536]{1,0:T(8,128)(2,1)}, bf16[2,16,48,768]{3,2,1,0:T(8,128)(2,1)}, bf16[2,16,48,768]{3,2,1,0:T(8,128)(2,1)}) custom-call(f32[128,1536]{1,0:T(8,128)} %copy-done.12, bf16[2,128,1536]{2,1,0:T(8,128)(2,1)} %get-tuple-element.82.active, f32[2,1536]{1,0:T(2,128)} %d_skip.3, ...), custom_call_target="tpu_custom_call" | custom-call | tf_op jit(solution)/shard_map/mid/pallas_call | solution.py:831
  126.0 18.3 %post.1 = (f32[144,768]{1,0:T(8,128)}, f32[8,2304]{1,0:T(8,128)}, bf16[2,16,48,512]{3,2,1,0:T(8,128)(2,1)}, bf16[2,16,48,640]{3,2,1,0:T(8,128)(2,1)}) custom-call(f32[2,128,1536]{2,1,0:T(8,128)} %copy-done.7, f32[2,128,1536]{2,1,0:T(8,128)} %copy-done.8, f32[2,128,256]{2,1,0:T(8,128)} %copy-done.16, f32[2,128,256]{2,1,0:T(8,128)} %copy-done.15, ...), custom_call_target="tpu_custom_call" | custom-call | tf_op jit(solution)/shard_map/post/pallas_call | solution.py:1029
  144.3 1.5 copy-done.3
  145.8 1.0 copy-done.6
  146.8 1.4 copy-done.9
  148.3 0.9 copy-done.21
  149.1 66.5 %reduce_shares.1 = (f32[48,768]{1,0:T(8,128)S(1)}, f32[48,768]{1,0:T(8,128)S(1)}, f32[48,512]{1,0:T(8,128)S(1)}, f32[48,640]{1,0:T(8,128)S(1)}, f32[8,2304]{1,0:T(8,128)S(1)}, /*index=5*/f32[16,768]{1,0:T(8,128)S(1)}) custom-call(bf16[2,16,48,768]{3,2,1,0:T(8,128)(2,1)} %get-tuple-element.89.refs_0_, bf16[2,16,48,768]{3,2,1,0:T(8,128)(2,1)} %get-tuple-element.90.refs_1_, ...), custom_call_target="tpu_custom_call" | custom-call | tf_op jit(solution)/shard_map/reduce_shares/pallas_call | solution.py:1203
  215.7 1.5 finish.1
  (35 shorter events, 0.6 us)
Async XLA Ops:
  1.4 7.9 %collective-permute-start = (bf16[8,768]{1,0:T(8,128)(2,1)S(1)}, bf16[8,768]{1,0:T(8,128)(2,1)S(1)}, u32[]{:S(2)}, u32[]{:S(2)}) collective-permute-start(bf16[8,768]{1,0:T(8,128)(2,1)S(1)} %get-tuple-element.134), channel_id=1, source_target_pairs={{0,1},{1,2},{2,3},{3,4},{4,5},{5,6},{6,7},{7,8},{8,9},{9,10},{10,1... | collective-permute-start | bytes 36872 | tf_op jit(solution)/shard_map/ppermute | solution.py:1338
  3.7 5.6 %collective-permute-start.1 = (bf16[8,768]{1,0:T(8,128)(2,1)S(1)}, bf16[8,768]{1,0:T(8,128)(2,1)S(1)}, u32[]{:S(2)}, u32[]{:S(2)}) collective-permute-start(bf16[8,768]{1,0:T(8,128)(2,1)S(1)} %get-tuple-element.133), channel_id=1, source_target_pairs={{1,0},{2,1},{3,2},{4,3},{5,4},{6,5},{7,6},{8,7},{9,8},{10,9},{11,1... | collective-permute-start | bytes 36872 | tf_op jit(solution)/shard_map/ppermute | solution.py:1339
  9.3 0.6 copy-start.23
  9.9 0.6 copy-start.24
  40.2 1.0 copy-start.14
  41.1 0.9 copy-start.18
  63.0 1.1 copy-start
  64.1 1.4 copy-start.1
  65.6 1.4 copy-start.2
  67.0 0.9 copy-start.10
  67.9 0.9 copy-start.20
  68.8 22.7 %copy-start.11 = (f32[2,16,1536]{2,1,0:T(8,128)S(1)}, f32[2,16,1536]{2,1,0:T(8,128)}, u32[]{:S(2)}) copy-start(f32[2,16,1536]{2,1,0:T(8,128)} %get-tuple-element.78.rate) | copy-start | bytes 589828
  68.8 22.7 %copy-start.19 = (bf16[2,128,256]{2,1,0:T(8,128)(2,1)S(1)}, bf16[2,128,256]{2,1,0:T(8,128)(2,1)}, u32[]{:S(2)}) copy-start(bf16[2,128,256]{2,1,0:T(8,128)(2,1)} %get-tuple-element.92.in_blk) | copy-start | bytes 393220
  90.6 0.9 copy-start.12
  91.5 22.2 %copy-start.15 = (f32[2,128,256]{2,1,0:T(8,128)}, f32[2,128,256]{2,1,0:T(8,128)S(1)}, u32[]{:S(2)}) copy-start(f32[2,128,256]{2,1,0:T(8,128)S(1)} %get-tuple-element.97.out_acc) | copy-start | bytes 786436
  113.7 1.2 copy-start.7
  115.0 1.2 copy-start.8
  116.2 0.7 copy-start.16
  116.9 0.7 copy-start.17
  144.3 1.5 copy-start.3
  145.8 1.0 copy-start.6
  146.8 1.4 copy-start.9
  148.3 0.9 copy-start.21
  149.1 66.6 %copy-start.4 = (f32[144,768]{1,0:T(8,128)S(1)}, f32[144,768]{1,0:T(8,128)}, u32[]{:S(2)}) copy-start(f32[144,768]{1,0:T(8,128)} %get-tuple-element.106.normed) | copy-start | bytes 1327108
  149.1 66.6 %copy-start.5 = (bf16[128,768]{1,0:T(8,128)(2,1)S(1)}, bf16[128,768]{1,0:T(8,128)(2,1)}, u32[]{:S(2)}) copy-start(bf16[128,768]{1,0:T(8,128)(2,1)} %grad_out.5) | copy-start | bytes 589828
  149.1 66.6 %copy-start.13 = (f32[128,768]{1,0:T(8,128)S(1)}, f32[128,768]{1,0:T(8,128)}, u32[]{:S(2)}) copy-start(f32[128,768]{1,0:T(8,128)} %get-tuple-element.120.scale1) | copy-start | bytes 1179652
  149.1 66.6 %copy-start.22 = (f32[128,128]{1,0:T(8,128)S(1)}, f32[128,128]{1,0:T(8,128)}, u32[]{:S(2)}) copy-start(f32[128,128]{1,0:T(8,128)} %get-tuple-element.119.rescale) | copy-start | bytes 196612

commit v2 on v1

--- a/solution.py
+++ b/solution.py
@@ -563,11 +563,29 @@
     return entering.reshape(2, rows // 2, 2, states, LANES)
 
 
-def states_kernel(masked, driven, seed, in_spread, out_blk, rate, entering, mixed, out_grad, kept):
+def pipelined(chunks, compute, finish, carry):
+    carry = compute(0, 0, carry)
+
+    def pair(i, carry):
+        carry = compute(2 * i + 1, 1, carry)
+        finish(2 * i, 0)
+        carry = compute(2 * i + 2, 0, carry)
+        finish(2 * i + 1, 1)
+        return carry
+
+    carry = lax.fori_loop(0, chunks // 2 - 1, pair, carry)
+    carry = compute(chunks - 1, 1, carry)
+    finish(chunks - 2, 0)
+    finish(chunks - 1, 1)
+    return carry
+
+
+def states_kernel(masked, driven, seed, in_spread, out_blk, rate, entering, mixed, out_grad, kept, r00, r01, r10, r11):
     tokens, cols = seed.shape
     per = cols // LANES
     states = rate.shape[1]
     chunks = tokens // CHUNK
+    rows = ((r00, r01), (r10, r11))
 
     @pl.when(pl.program_id(0) == 0)
     def _():
@@ -579,13 +597,14 @@
         kept[0, 0:states, lanes] = entering[0, c, 0]
         kept[1, tokens * states : (tokens + 1) * states, lanes] = entering[1, c, 1]
 
-    def forward(i, carry):
+    def first_of(d, i):
+        return pl.multiple_of((i if d == 0 else chunks - 1 - i) * CHUNK, CHUNK)
+
+    def compute(i, side, carry):
         carry = list(carry)
-        for d in range(2):
-            first = pl.multiple_of((i if d == 0 else chunks - 1 - i) * CHUNK, CHUNK)
-            slot = pl.multiple_of((first + 1 - d) * states, states)
-            block = kept.at[d, pl.ds(slot, CHUNK * states), :]
-            for k in range(CHUNK):
+        for k in range(CHUNK):
+            for d in range(2):
+                first = first_of(d, i)
                 j = k if d == 0 else CHUNK - 1 - k
                 in_row = in_spread[d, first + j]
                 for c in range(per):
@@ -594,15 +613,22 @@
                     state = now * carry[d * per + c] + in_row * row_of(
                         driven.at[d], first, j, lanes
                     )
-                    block[j * states : (j + 1) * states, lanes] = state.astype(BF16)
+                    rows[side][d][j * states : (j + 1) * states, lanes] = state.astype(BF16)
                     carry[d * per + c] = state
+        return tuple(carry)
+
+    def finish(i, side):
+        for d in range(2):
+            first = first_of(d, i)
             here = pl.ds(first, CHUNK)
-            mixed[here, :] += dot(out_blk[d, here, :], block[...])
-            out_grad[d, here, :] += contract_cols(seed[here, :].astype(BF16), block[...])
-        return tuple(carry)
+            slot = pl.multiple_of((first + 1 - d) * states, states)
+            block = rows[side][d][...]
+            kept[d, pl.ds(slot, CHUNK * states), :] = block
+            mixed[here, :] += dot(out_blk[d, here, :], block)
+            out_grad[d, here, :] += contract_cols(seed[here, :].astype(BF16), block)
 
     start = tuple(entering[d, c, d].astype(F32) for d in range(2) for c in range(per))
-    lax.fori_loop(0, chunks, forward, start)
+    pipelined(chunks, compute, finish, start)
 
 
 def block_specs(tokens, states):
@@ -632,118 +658,10 @@
             shaped((2, tokens, CHUNK * states)),
             shaped((2, (tokens + 1) * states, inner), BF16),
         ],
+        scratch_shapes=[pltpu.VMEM((CHUNK * states, COLS), BF16)] * 4,
         compiler_params=pltpu.CompilerParams(vmem_limit_bytes=48 * MIB),
         name="states",
     )(h["masked"], h["driven"], h["seed"], h["in_spread"], h["out_blk"], h["rate"], entering)
-
-
-def adjoints_kernel(
-    masked,
-    driven,
-    seed,
-    out_spread,
-    in_blk,
-    rate,
-    entering,
-    kept,
-    decay_grad,
-    driven_grad,
-    in_grad,
-    rate_grad,
-    rows_a,
-    rows_b,
-    rows_c,
-    rows_d,
-):
-    tokens, cols = seed.shape
-    per = cols // LANES
-    states = rate.shape[1]
-    chunks = tokens // CHUNK
-    wide = CHUNK * states
-    ones = (
-        lax.broadcasted_iota(jnp.int32, (CHUNK, wide), 1) // states
-        == lax.broadcasted_iota(jnp.int32, (CHUNK, wide), 0)
-    ).astype(BF16)
-
-    @pl.when(pl.program_id(0) == 0)
-    def _():
-        in_grad[...] = jnp.zeros_like(in_grad)
-
-    def backward(i, carry):
-        carry = list(carry)
-        for d in range(2):
-            first = pl.multiple_of((chunks - 1 - i if d == 0 else i) * CHUNK, CHUNK)
-            slot = pl.multiple_of((first + d) * states, states)
-            before = kept.at[d, pl.ds(slot, wide), :]
-            adjs = (rows_a, rows_b)[d]
-            slopes = (rows_c, rows_d)[d]
-            for k in range(CHUNK):
-                j = CHUNK - 1 - k if d == 0 else k
-                out_row = out_spread[d, first + j]
-                part = slice(j * states, (j + 1) * states)
-                for c in range(per):
-                    lanes = pl.ds(c * LANES, LANES)
-                    coming, total = carry[d * per + c]
-                    step = row_of(masked.at[d], first, j, lanes)
-                    now = jnp.exp2(step * rate[d, :, lanes])
-                    adj = out_row * row_of(seed, first, j, lanes) + coming
-                    coming = now * adj
-                    slope = coming * before[part, lanes].astype(F32) * rate[d, :, lanes]
-                    total = total + slope * step
-                    adjs[part, lanes] = adj.astype(BF16)
-                    slopes[part, lanes] = slope.astype(BF16)
-                    carry[d * per + c] = (coming, total)
-            here = pl.ds(first, CHUNK)
-            driven_grad[d, here, :] = dot(in_blk[d, here, :], adjs[...])
-            in_grad[d, here, :] += contract_cols(driven[d, here, :].astype(BF16), adjs[...])
-            decay_grad[d, here, :] = dot(ones, slopes[...]) * LN2
-        return tuple(carry)
-
-    zero = jnp.zeros((states, LANES), F32)
-    start = tuple((entering[d, c, 1 - d].astype(F32), zero) for d in range(2) for c in range(per))
-    carry = lax.fori_loop(0, chunks, backward, start)
-    for d in range(2):
-        for c in range(per):
-            rate_grad[d, :, c * LANES : (c + 1) * LANES] = carry[d * per + c][1] * LN2
-
-
-def run_adjoints(h, entering, kept):
-    tokens, inner = h["seed"].shape
-    states = h["rate"].shape[1]
-    s = block_specs(tokens, states)
-    return pl.pallas_call(
-        adjoints_kernel,
-        grid=(inner // COLS,),
-        in_specs=[
-            s["both"],
-            s["both"],
-            s["rows"],
-            s["spread"],
-            s["diag"],
-            s["rate"],
-            s["entering"],
-            s["kept"],
-        ],
-        out_specs=[s["both"], s["both"], s["diag"], s["rate"]],
-        out_shape=[
-            shaped((2, tokens, inner)),
-            shaped((2, tokens, inner)),
-            shaped((2, tokens, CHUNK * states)),
-            shaped((2, states, inner)),
-        ],
-        scratch_shapes=[pltpu.VMEM((CHUNK * states, COLS), BF16)] * 4,
-        compiler_params=pltpu.CompilerParams(vmem_limit_bytes=48 * MIB),
-        name="adjoints",
-    )(
-        h["masked"],
-        h["driven"],
-        h["seed"],
-        h["out_spread"],
-        h["in_blk"],
-        h["rate"],
-        entering,
-        kept,
-    )
 
 
 def slot_of(o, count, order):
@@ -863,84 +781,298 @@
     )
 
 
-def post_kernel(
-    count,
-    decay_grad,
-    driven_grad,
-    in_acc,
-    out_acc,
-    rate_grad,
-    logit,
-    active,
-    rank_low,
-    seed,
-    conv_sum,
-    conv_keep,
-    masks,
-    hot,
-    d_skip,
-    conv_w,
-    mixer,
-    normed,
-    gate_grad,
-    gate_branch_grad,
-    w_x,
-    w_dt,
-    w_in,
-    norm_wide,
-    mod_part,
-    slots_a,
-    slots_b,
-    active_grad,
-    rank_grad,
-    proj_grad,
-    conv_wide,
-    input_wide,
-    whole_conv,
-    whole_cols,
-    small,
-    stage,
-):
-    tokens, inner = seed.shape
-    model = normed.shape[1]
-    wide = normed.shape[0]
-    taps = conv_w.shape[1]
-    rank = w_dt.shape[1]
-    proj = w_x.shape[2]
-    states = rate_grad.shape[1]
-    seqs = mod_part.shape[0]
-    rank_grad[...] = jnp.zeros_like(rank_grad)
-    small[...] = jnp.zeros_like(small)
-    at_conv, at_bias, at_dt, at_skip, at_rate = (
-        0,
-        2 * taps,
-        2 * taps + 2,
-        2 * taps + 4,
-        2 * taps + 8,
-    )
-
-    def column_sum(values):
-        return jnp.sum(values, axis=0, keepdims=True)
-
-    def through_steps(b, none):
+class Place:
+    def __init__(self, count):
+        self.count = count
+        self.groups = count // PLANE
+        self.me = lax.axis_index("seq")
+        self.bits = [lax.rem(self.me, 2), lax.rem(self.me // 2, 2), lax.rem(self.me // 4, 2)]
+        self.flips = [self.me + (1 - 2 * self.bits[i]) * (1 << i) for i in range(3)]
+        self.level = self.me // PLANE
+        self.low = lax.rem(self.me, PLANE)
+        self.left = lax.rem(self.me + count - 1, count)
+        self.right = lax.rem(self.me + 1, count)
+        self.far = [lax.rem(self.level + k, self.groups) for k in range(1, self.groups)]
+
+    def meet(self):
+        barrier = pltpu.get_barrier_semaphore()
+        peers = self.flips + [self.left, self.right] + [g * PLANE + self.low for g in self.far]
+        for peer in peers:
+            pl.semaphore_signal(barrier, inc=1, device_id=(peer,), device_id_type=MESH)
+        pl.semaphore_wait(barrier, len(peers))
+
+
+def remote(src, dst, sems, slot, peer):
+    return pltpu.make_async_remote_copy(
+        src_ref=src,
+        dst_ref=dst,
+        send_sem=sems[0].at[slot],
+        recv_sem=sems[1].at[slot],
+        device_id=(peer,),
+        device_id_type=MESH,
+    )
+
+
+def add_into(into, own, first):
+    def one(i, none):
+        into[i] = into[i] + own[first + i]
+        return none
+
+    lax.fori_loop(0, into.shape[0], one, 0)
+
+
+class Halving:
+    def __init__(self, place, orders, parts, owns, got, sems):
+        self.place, self.orders, self.parts, self.owns = place, orders, parts, owns
+        self.got1, self.got2, self.got3, self.got4 = got
+        self.sems = sems
+        self.number = len(orders)
+
+    def turns(self, p):
+        return (1, 2) if self.orders[p] == "xy" else (2, 1)
+
+    def first(self, p):
+        bit = self.place.bits[0]
+        return remote(
+            self.parts[p].at[1 - bit], self.got1[p], self.sems, p, self.place.flips[0]
+        )
+
+    def second(self, p):
+        i, _ = self.turns(p)
+        half = 2 * self.place.groups
+        src = self.got1[p].at[pl.ds((1 - self.place.bits[i]) * half, half)]
+        return remote(src, self.got2[p], self.sems, self.number + p, self.place.flips[i])
+
+    def third(self, p):
+        _, j = self.turns(p)
+        half = self.place.groups
+        src = self.got2[p].at[pl.ds((1 - self.place.bits[j]) * half, half)]
+        return remote(src, self.got3[p], self.sems, 2 * self.number + p, self.place.flips[j])
+
+    def fourth(self, p):
+        copies = []
+        for k, g in enumerate(self.place.far):
+            slot = 3 * self.number + p * len(self.place.far) + k
+            copies.append(
+                remote(
+                    self.got3[p].at[g],
+                    self.got4[p].at[self.place.level],
+                    self.sems,
+                    slot,
+                    g * PLANE + self.place.low,
+                )
+            )
+        return copies
+
+    def start(self, p):
+        self.first(p).start()
+
+    def step2(self, p):
+        self.first(p).wait_recv()
+        add_into(self.got1[p], self.owns[p], 0)
+        self.second(p).start()
+
+    def step3(self, p):
+        i, _ = self.turns(p)
+        self.second(p).wait_recv()
+        add_into(self.got2[p], self.got1[p], self.place.bits[i] * 2 * self.place.groups)
+        self.third(p).start()
+
+    def step4(self, p):
+        _, j = self.turns(p)
+        self.third(p).wait_recv()
+        add_into(self.got3[p], self.got2[p], self.place.bits[j] * self.place.groups)
+        for copy in self.fourth(p):
+            copy.start()
+        self.got4[p][self.place.level] = self.got3[p][self.place.level]
+
+    def end(self, p, share):
+        for copy in self.fourth(p):
+            copy.wait_recv()
+        total = self.got4[p][0].astype(F32)
+        for g in range(1, self.place.groups):
+            total = total + self.got4[p][g].astype(F32)
+        share[...] = total
+        for copy in [self.first(p), self.second(p), self.third(p)] + self.fourth(p):
+            copy.wait_send()
+
+    def all(self, step):
+        for p in range(self.number):
+            getattr(self, step)(p)
+
+
+def halving_sems(number, groups):
+    return [pltpu.SemaphoreType.DMA((3 * number + number * (groups - 1),))] * 2
+
+
+def halving_slots(shapes, groups):
+    return [
+        pltpu.VMEM((size,) + shape, BF16)
+        for size in (4 * groups, 2 * groups, groups, groups)
+        for shape in shapes
+    ]
+
+
+BLOCKED = ("masked", "driven", "seed", "rate", "entering", "kept")
+FIXED = ("out_spread", "in_blk", "d_skip", "conv_w")
+FETCHED = (
+    "out_acc",
+    "rank_low",
+    "w_dt",
+    "logit",
+    "active",
+    "seed_all",
+    "w_x",
+    "conv_sum",
+    "conv_keep",
+    "masks",
+    "mixer",
+    "w_in",
+    "gate_branch_grad",
+    "hot",
+    "normed",
+    "gate_grad",
+)
+BACK_OUT = ("norm_wide", "share_out", "share_gate", "share_a", "share_b", "mod", "edges")
+BACK_SCRATCH = (
+    "decay_grad",
+    "driven_grad",
+    "in_acc",
+    "small",
+    "adj00",
+    "adj01",
+    "adj10",
+    "adj11",
+    "slope00",
+    "slope01",
+    "slope10",
+    "slope11",
+    "active_grad",
+    "rank_grad",
+    "proj_grad",
+    "conv_wide",
+    "input_wide",
+    "whole_conv",
+    "whole_cols",
+    "stage",
+    "late_a",
+    "late_b",
+    "mod_part",
+    "m1",
+    "m2",
+    "m3",
+    "m4",
+    "edge_got",
+    "own_out",
+    "own_gate",
+)
+
+
+class Refs:
+    def __init__(self, names, refs):
+        for name, ref in zip(names, refs):
+            setattr(self, name, ref)
+
+
+def small_rows(taps):
+    return 0, 2 * taps, 2 * taps + 2, 2 * taps + 4, 2 * taps + 8
+
+
+def adjoint_block(r, b):
+    tokens, cols = r.seed.shape
+    per = cols // LANES
+    states = r.rate.shape[1]
+    taps = r.conv_w.shape[1]
+    chunks = tokens // CHUNK
+    wide = CHUNK * states
+    adjs = ((r.adj00, r.adj01), (r.adj10, r.adj11))
+    slopes = ((r.slope00, r.slope01), (r.slope10, r.slope11))
+    at_cols = pl.ds(pl.multiple_of(b * cols, cols), cols)
+    ones = (
+        lax.broadcasted_iota(jnp.int32, (CHUNK, wide), 1) // states
+        == lax.broadcasted_iota(jnp.int32, (CHUNK, wide), 0)
+    ).astype(BF16)
+
+    def first_of(d, i):
+        return pl.multiple_of((chunks - 1 - i if d == 0 else i) * CHUNK, CHUNK)
+
+    def compute(i, side, carry):
+        carry = list(carry)
+        for k in range(CHUNK):
+            for d in range(2):
+                first = first_of(d, i)
+                slot = pl.multiple_of((first + d) * states, states)
+                before = r.kept.at[d, pl.ds(slot, wide), :]
+                j = CHUNK - 1 - k if d == 0 else k
+                out_row = r.out_spread[d, first + j]
+                part = slice(j * states, (j + 1) * states)
+                for c in range(per):
+                    lanes = pl.ds(c * LANES, LANES)
+                    coming, total = carry[d * per + c]
+                    step = row_of(r.masked.at[d], first, j, lanes)
+                    now = jnp.exp2(step * r.rate[d, :, lanes])
+                    adj = out_row * row_of(r.seed, first, j, lanes) + coming
+                    coming = now * adj
+                    slope = coming * before[part, lanes].astype(F32) * r.rate[d, :, lanes]
+                    total = total + slope * step
+                    adjs[side][d][part, lanes] = adj.astype(BF16)
+                    slopes[side][d][part, lanes] = slope.astype(BF16)
+                    carry[d * per + c] = (coming, total)
+        return tuple(carry)
+
+    def finish(i, side):
+        for d in range(2):
+            here = pl.ds(first_of(d, i), CHUNK)
+            block = adjs[side][d][...]
+            r.driven_grad[d, here, at_cols] = dot(r.in_blk[d, here, :], block)
+            r.in_acc[d, here, :] += contract_cols(r.driven[d, here, :].astype(BF16), block)
+            r.decay_grad[d, here, at_cols] = dot(ones, slopes[side][d][...]) * LN2
+
+    zero = jnp.zeros((states, LANES), F32)
+    start = tuple(
+        (r.entering[d, c, 1 - d].astype(F32), zero) for d in range(2) for c in range(per)
+    )
+    carry = pipelined(chunks, compute, finish, start)
+    at_rate = small_rows(taps)[4]
+    for d in range(2):
+        for c in range(per):
+            lanes = tile_at(b * cols + c * LANES)
+            r.small[at_rate + d * states : at_rate + (d + 1) * states, lanes] = (
+                carry[d * per + c][1] * LN2
+            )
+
+
+def column_sum(values):
+    return jnp.sum(values, axis=0, keepdims=True)
+
+
+def through_steps(r):
+    tokens, inner = r.seed_all.shape
+    taps = r.conv_w.shape[1]
+    rank = r.w_dt.shape[1]
+    proj = r.w_x.shape[2]
+    states = r.rate.shape[1]
+    _, _, at_dt, at_skip, _ = small_rows(taps)
+    r.rank_grad[...] = jnp.zeros_like(r.rank_grad)
+
+    def block(b, none):
         cols = pl.ds(pl.multiple_of(b * COLS, COLS), COLS)
         for d in range(2):
-            act = active[d, :, cols].astype(F32)
-            value = logit[d, :, cols]
-            back = driven_grad[d, :, cols]
-            grown = seed[:, cols]
-            grad = (decay_grad[d, :, cols] + back * act) * sigmoid(value)
+            act = r.active[d, :, cols].astype(F32)
+            value = r.logit[d, :, cols]
+            back = r.driven_grad[d, :, cols]
+            grown = r.seed_all[:, cols]
+            grad = (r.decay_grad[d, :, cols] + back * act) * sigmoid(value)
             low = grad.astype(BF16)
-            active_grad[d, :, cols] = back * softplus(value) + grown * d_skip[d : d + 1, cols]
-            small[at_dt + d : at_dt + d + 1, cols] = column_sum(grad)
-            small[at_skip + d : at_skip + d + 1, cols] = column_sum(grown * act)
-            small[at_rate + d * states : at_rate + (d + 1) * states, cols] = rate_grad[d, :, cols]
-            rank_grad[d] += contract_cols(low, w_dt[d, :, cols])
+            r.active_grad[d, :, cols] = back * softplus(value) + grown * r.d_skip[d : d + 1, cols]
+            r.small[at_dt + d : at_dt + d + 1, cols] = column_sum(grad)
+            r.small[at_skip + d : at_skip + d + 1, cols] = column_sum(grown * act)
+            r.rank_grad[d] += contract_cols(low, r.w_dt[d, :, cols])
             start = 2 * proj + d * rank
-            whole_cols[cols, start : start + rank] = contract_rows(low, rank_low[d])
+            r.whole_cols[cols, start : start + rank] = contract_rows(low, r.rank_low[d])
         return none
 
-    lax.fori_loop(0, inner // COLS, through_steps, 0)
+    lax.fori_loop(0, inner // COLS, block, 0)
 
     place = lax.rem(lax.broadcasted_iota(jnp.int32, (tokens, CHUNK * states), 0), CHUNK)
     owner = lax.broadcasted_iota(jnp.int32, (tokens, CHUNK * states), 1) // states
@@ -948,64 +1080,220 @@
     column = lax.rem(lax.broadcasted_iota(jnp.int32, (CHUNK * states, states), 0), states)
     gather = (column == lax.broadcasted_iota(jnp.int32, (CHUNK * states, states), 1)).astype(BF16)
     for d in range(2):
-        proj_grad[d, :, 0:rank] = rank_grad[d].astype(BF16)
-        for start, acc in ((rank, in_acc), (rank + states, out_acc)):
+        r.proj_grad[d, :, 0:rank] = r.rank_grad[d].astype(BF16)
+        for start, acc in ((rank, r.in_acc), (rank + states, r.out_acc)):
             kept = jnp.where(on_diag, acc[d], 0.0).astype(BF16)
-            proj_grad[d, :, start : start + states] = dot(kept, gather).astype(BF16)
-
-    norm_wide[...] = jnp.zeros_like(norm_wide)
-
-    def through_conv(b, none):
+            r.proj_grad[d, :, start : start + states] = dot(kept, gather).astype(BF16)
+
+
+def through_conv(r):
+    tokens, inner = r.seed_all.shape
+    taps = r.conv_w.shape[1]
+    rank = r.w_dt.shape[1]
+    proj = r.w_x.shape[2]
+    at_conv, at_bias, _, _, _ = small_rows(taps)
+    r.norm_wide[...] = jnp.zeros_like(r.norm_wide)
+
+    def block(b, none):
         cols = pl.ds(pl.multiple_of(b * COLS, COLS), COLS)
-        conv_wide[...] = conv_keep[:, cols].astype(F32)
-        input_wide[...] = jnp.zeros_like(input_wide)
+        r.conv_wide[...] = r.conv_keep[:, cols].astype(F32)
+        r.input_wide[...] = jnp.zeros_like(r.input_wide)
         for d in range(2):
-            low = proj_grad[d]
+            low = r.proj_grad[d]
             start = d * proj
-            whole_cols[cols, start : start + proj] = contract_rows(active[d, :, cols], low)
-            total = active_grad[d, :, cols] + contract_cols(low, w_x[d, cols, :])
+            r.whole_cols[cols, start : start + proj] = contract_rows(r.active[d, :, cols], low)
+            total = r.active_grad[d, :, cols] + contract_cols(low, r.w_x[d, cols, :])
             for c in range(COLS // LANES):
                 lanes = tile_at(b * COLS + c * LANES)
                 here = slice(c * LANES, (c + 1) * LANES)
-                grad = total[:, here] * silu_slope(conv_sum[d, :, lanes])
-                small[at_bias + d : at_bias + d + 1, lanes] = column_sum(grad)
+                grad = total[:, here] * silu_slope(r.conv_sum[d, :, lanes])
+                r.small[at_bias + d : at_bias + d + 1, lanes] = column_sum(grad)
                 for k in range(taps):
                     offset = offset_of(d, k, taps)
                     window = slice(RIM + offset, RIM + offset + tokens)
-                    part = grad * masks[offset + taps - 1]
+                    part = grad * r.masks[offset + taps - 1]
                     at = at_conv + d * taps + k
-                    small[at : at + 1, lanes] = column_sum(part * conv_wide[window, here])
-                    input_wide[window, here] += conv_w[d, k : k + 1, lanes] * part
-        low = input_wide[...].astype(BF16)
-        whole_conv[:, cols] = contract_rows(mixer[...], low)
-        norm_wide[...] += contract_cols(low, w_in[:, cols])
+                    r.small[at : at + 1, lanes] = column_sum(part * r.conv_wide[window, here])
+                    r.input_wide[window, here] += r.conv_w[d, k : k + 1, lanes] * part
+        low = r.input_wide[...].astype(BF16)
+        r.whole_conv[:, cols] = contract_rows(r.mixer[...], low)
+        r.norm_wide[...] += contract_cols(low, r.w_in[:, cols])
         gate_cols = pl.ds(pl.multiple_of(inner + b * COLS, COLS), COLS)
-        norm_wide[RIM : RIM + tokens, :] += contract_cols(
-            gate_branch_grad[:, cols], w_in[:, gate_cols]
+        r.norm_wide[RIM : RIM + tokens, :] += contract_cols(
+            r.gate_branch_grad[:, cols], r.w_in[:, gate_cols]
         )
-        whole_cols[cols, 2 * (proj + rank) :] = small[:, cols].T
+        r.whole_cols[cols, 2 * (proj + rank) :] = r.small[:, cols].T
         return none
 
-    lax.fori_loop(0, inner // COLS, through_conv, 0)
-
-    seq_rows = hot[:, 0:seqs]
-    grads = norm_wide[...]
-    mod_part[:, 0:model] = contract_rows(seq_rows, grads, HIGHEST)
-    mod_part[:, model : 2 * model] = contract_rows(seq_rows, grads * normed[...], HIGHEST)
-    mod_part[:, 2 * model :] = contract_rows(
-        hot[RIM : RIM + tokens, 0:seqs], gate_grad[...], HIGHEST
-    )
-
+    lax.fori_loop(0, inner // COLS, block, 0)
+
+
+def fill_slots(r, count):
+    inner = r.seed_all.shape[1]
+    model = r.normed.shape[1]
     rows, mrows = inner // count, model // count
-    cut = slots_a.shape[3]
+    cut = r.late_a.shape[3]
     rest = model - cut
     for o in range(count):
-        both = stacked_rows(whole_conv, stage, o, mrows).astype(BF16)
+        both = stacked_rows(r.whole_conv, r.stage, o, mrows).astype(BF16)
         first, later = slot_of(o, count, "xy")
-        slots_a[first, later] = both[:, :cut]
+        r.late_a[first, later] = both[:, :cut]
         first, later = slot_of(o, count, "yx")
-        slots_b[first, later, :, 0:rest] = both[:, cut:]
-        slots_b[first, later, 0:rows, rest:] = whole_cols[o * rows : (o + 1) * rows, :].astype(BF16)
+        r.late_b[first, later, :, 0:rest] = both[:, cut:]
+        r.late_b[first, later, 0:rows, rest:] = r.whole_cols[o * rows : (o + 1) * rows, :].astype(
+            BF16
+        )
+
+
+def modulation_sums(r):
+    tokens = r.seed_all.shape[0]
+    model = r.normed.shape[1]
+    seqs = r.mod_part.shape[0]
+    seq_rows = r.hot[:, 0:seqs]
+    grads = r.norm_wide[...]
+    r.mod_part[:, 0:model] = contract_rows(seq_rows, grads, HIGHEST)
+    r.mod_part[:, model : 2 * model] = contract_rows(seq_rows, grads * r.normed[...], HIGHEST)
+    r.mod_part[:, 2 * model :] = contract_rows(
+        r.hot[RIM : RIM + tokens, 0:seqs], r.gate_grad[...], HIGHEST
+    )
+
+
+def back_kernel(count, *refs):
+    refs = list(refs)
+
+    def take(size):
+        taken = refs[:size]
+        del refs[:size]
+        return taken
+
+    blocked, fixed = take(len(BLOCKED)), take(len(FIXED))
+    early = take(2)
+    sources = take(len(FETCHED))
+    out = take(len(BACK_OUT))
+    scratch = take(len(BACK_SCRATCH))
+    fetched = take(len(FETCHED))
+    early_got = [take(2) for _ in range(4)]
+    late_got = [take(2) for _ in range(4)]
+    early_sems, late_sems, mod_sems = take(2), take(2), take(2)
+    fetch_sems, own_sems = take(2)
+    r = Refs(
+        BLOCKED + FIXED + BACK_OUT + BACK_SCRATCH + FETCHED,
+        blocked + fixed + out + scratch + fetched,
+    )
+    b = pl.program_id(0)
+    blocks = pl.num_programs(0)
+    place = Place(count)
+    orders = ("xy", "yx")
+    owns = (r.own_out, r.own_gate)
+    one = Halving(place, orders, early, owns, early_got, early_sems)
+    two = Halving(
+        place,
+        orders,
+        (r.late_a, r.late_b),
+        (r.late_a.at[place.bits[0]], r.late_b.at[place.bits[0]]),
+        late_got,
+        late_sems,
+    )
+
+    def fetch(i):
+        return pltpu.make_async_copy(sources[i], fetched[i], fetch_sems.at[i])
+
+    def own(p):
+        return pltpu.make_async_copy(early[p].at[place.bits[0]], owns[p], own_sems.at[p])
+
+    @pl.when(b == 0)
+    def _():
+        place.meet()
+        one.all("start")
+        for p in range(2):
+            own(p).start()
+        for i in range(len(FETCHED)):
+            fetch(i).start()
+        r.in_acc[...] = jnp.zeros_like(r.in_acc)
+        r.small[...] = jnp.zeros_like(r.small)
+
+    adjoint_block(r, b)
+
+    @pl.when(b == 0)
+    def _():
+        for p in range(2):
+            own(p).wait()
+        one.all("step2")
+
+    @pl.when(b == blocks - 2)
+    def _():
+        one.all("step3")
+
+    @pl.when(b == blocks - 1)
+    def _():
+        for i in range(len(FETCHED)):
+            fetch(i).wait()
+        through_steps(r)
+        one.all("step4")
+        through_conv(r)
+        fill_slots(r, count)
+        two.all("start")
+        far = len(place.far)
+        edges = [
+            remote(
+                r.norm_wide.at[pl.ds(0, RIM)],
+                r.edge_got.at[pl.ds(RIM, RIM)],
+                mod_sems,
+                3 + far,
+                place.left,
+            ),
+            remote(
+                r.norm_wide.at[pl.ds(r.norm_wide.shape[0] - RIM, RIM)],
+                r.edge_got.at[pl.ds(0, RIM)],
+                mod_sems,
+                4 + far,
+                place.right,
+            ),
+        ]
+        for copy in edges:
+            copy.start()
+        modulation_sums(r)
+        levels = ((r.mod_part, r.m1), (r.m1, r.m2), (r.m2, r.m3))
+        mods = [
+            remote(src, dst, mod_sems, i, place.flips[i]) for i, (src, dst) in enumerate(levels)
+        ]
+        last = [
+            remote(r.m3, r.m4.at[place.level], mod_sems, 3 + k, g * PLANE + place.low)
+            for k, g in enumerate(place.far)
+        ]
+
+        def mod_step(i):
+            mods[i].wait_recv()
+            levels[i][1][...] += levels[i][0][...]
+            if i < 2:
+                mods[i + 1].start()
+                return
+            for copy in last:
+                copy.start()
+            r.m4[place.level] = r.m3[...]
+
+        mods[0].start()
+        two.all("step2")
+        mod_step(0)
+        one.end(0, r.share_out)
+        one.end(1, r.share_gate)
+        two.step3(0)
+        mod_step(1)
+        two.step3(1)
+        two.step4(0)
+        mod_step(2)
+        two.step4(1)
+        for copy in last + edges:
+            copy.wait_recv()
+        r.edges[...] = r.edge_got[...]
+        total = r.m4[0]
+        for g in range(1, place.groups):
+            total = total + r.m4[g]
+        r.mod[...] = total
+        two.end(0, r.share_a)
+        two.end(1, r.share_b)
+        for copy in mods + last + edges:
+            copy.wait_send()
 
 
 def column_width(proj, rank, taps, states):
@@ -1015,210 +1303,101 @@
     return small + -total % LANES, total + -total % LANES
 
 
-def run_post(h, count, adjoint_side, out_acc, mid_side, d_skip, conv_w, w_x, w_dt, w_in):
-    decay_grad, driven_grad, in_acc, rate_grad = adjoint_side
-    gate_grad, gate_branch_grad = mid_side
+def once(shape):
+    return pl.BlockSpec(shape, lambda b: (0,) * len(shape), pipeline_mode=pl.Buffered(1))
+
+
+def run_back(h, count, entering, kept, out_acc, mid_side, d_skip, conv_w, w_x, w_dt, w_in):
+    gate_grad, gate_branch_grad, slots_out, slots_gate = mid_side
     tokens, inner = h["seed"].shape
     wide, model = h["normed"].shape
+    groups = count // PLANE
     rank = w_dt.shape[1]
     proj = w_x.shape[2]
-    states = rate_grad.shape[1]
+    states = h["rate"].shape[1]
     small, width = column_width(proj, rank, conv_w.shape[1], states)
     rows = slot_rows(count, inner)
     cut = (model + width) // 2 // LANES * LANES
+    far = groups - 1
+    given = dict(
+        h,
+        entering=entering,
+        kept=kept,
+        out_acc=out_acc,
+        seed_all=h["seed"],
+        gate_grad=gate_grad,
+        gate_branch_grad=gate_branch_grad,
+        d_skip=d_skip,
+        conv_w=conv_w,
+        w_x=w_x,
+        w_dt=w_dt,
+        w_in=w_in,
+    )
+    s = block_specs(tokens, states)
+    kinds = dict(masked="both", driven="both", seed="rows", rate="rate", entering="entering", kept="kept")
+    late = [(rows, cut), (rows, model + width - cut)]
+    early = [(rows, model)] * 2
+    diag = (CHUNK * states, COLS)
+    mod = (8, 3 * model)
+    scratch = dict(
+        decay_grad=pltpu.VMEM((2, tokens, inner), F32),
+        driven_grad=pltpu.VMEM((2, tokens, inner), F32),
+        in_acc=pltpu.VMEM((2, tokens, CHUNK * states), F32),
+        small=pltpu.VMEM((small, inner), F32),
+        active_grad=pltpu.VMEM((2, tokens, inner), F32),
+        rank_grad=pltpu.VMEM((2, tokens, rank), F32),
+        proj_grad=pltpu.VMEM((2, tokens, proj), BF16),
+        conv_wide=pltpu.VMEM((wide, COLS), F32),
+        input_wide=pltpu.VMEM((wide, COLS), F32),
+        whole_conv=pltpu.VMEM((model, inner), F32),
+        whole_cols=pltpu.VMEM((inner, width), F32),
+        stage=pltpu.VMEM((rows, model), F32),
+        late_a=pltpu.VMEM((2, 4 * groups) + late[0], BF16),
+        late_b=pltpu.VMEM((2, 4 * groups) + late[1], BF16),
+        mod_part=pltpu.VMEM(mod, F32),
+        m1=pltpu.VMEM(mod, F32),
+        m2=pltpu.VMEM(mod, F32),
+        m3=pltpu.VMEM(mod, F32),
+        m4=pltpu.VMEM((groups,) + mod, F32),
+        edge_got=pltpu.VMEM((2 * RIM, model), F32),
+        own_out=pltpu.VMEM((4 * groups,) + early[0], BF16),
+        own_gate=pltpu.VMEM((4 * groups,) + early[1], BF16),
+    )
+    outs = dict(
+        norm_wide=shaped((wide, model)),
+        share_out=shaped(early[0]),
+        share_gate=shaped(early[1]),
+        share_a=shaped(late[0]),
+        share_b=shaped(late[1]),
+        mod=shaped(mod),
+        edges=shaped((2 * RIM, model)),
+    )
     return pl.pallas_call(
-        functools.partial(post_kernel, count),
-        in_specs=[VMEM] * 22,
-        out_specs=[VMEM] * 4,
-        out_shape=[
-            shaped((wide, model)),
-            shaped((8, 3 * model)),
-            shaped((2, count // 2, rows, cut), BF16),
-            shaped((2, count // 2, rows, model + width - cut), BF16),
-        ],
-        scratch_shapes=[
-            pltpu.VMEM((2, tokens, inner), F32),
-            pltpu.VMEM((2, tokens, rank), F32),
-            pltpu.VMEM((2, tokens, proj), BF16),
-            pltpu.VMEM((wide, COLS), F32),
-            pltpu.VMEM((wide, COLS), F32),
-            pltpu.VMEM((model, inner), F32),
-            pltpu.VMEM((inner, width), F32),
-            pltpu.VMEM((small, inner), F32),
-            pltpu.VMEM((rows, model), F32),
-        ],
-        compiler_params=pltpu.CompilerParams(vmem_limit_bytes=58 * MIB),
-        name="post",
+        functools.partial(back_kernel, count),
+        grid=(inner // COLS,),
+        in_specs=[s[kinds[name]] for name in BLOCKED]
+        + [once(given[name].shape) for name in FIXED]
+        + [ANY] * (2 + len(FETCHED)),
+        out_specs=[once(outs[name].shape) for name in BACK_OUT],
+        out_shape=[outs[name] for name in BACK_OUT],
+        scratch_shapes=[scratch.get(name, pltpu.VMEM(diag, BF16)) for name in BACK_SCRATCH]
+        + [pltpu.VMEM(given[name].shape, given[name].dtype) for name in FETCHED]
+        + halving_slots(early, groups)
+        + halving_slots(late, groups)
+        + halving_sems(2, groups)
+        + halving_sems(2, groups)
+        + [pltpu.SemaphoreType.DMA((5 + far,))] * 2
+        + [pltpu.SemaphoreType.DMA((len(FETCHED),)), pltpu.SemaphoreType.DMA((2,))],
+        compiler_params=pltpu.CompilerParams(
+            collective_id=1, has_side_effects=True, vmem_limit_bytes=60 * MIB
+        ),
+        name="back",
     )(
-        decay_grad,
-        driven_grad,
-        in_acc,
-        out_acc,
-        rate_grad,
-        h["logit"],
-        h["active"],
-        h["rank_low"],
-        h["seed"],
-        h["conv_sum"],
-        h["conv_keep"],
-        h["masks"],
-        h["hot"],
-        d_skip,
-        conv_w,
-        h["mixer"],
-        h["normed"],
-        gate_grad,
-        gate_branch_grad,
-        w_x,
-        w_dt,
-        w_in,
-    )
-
-
-def reduce_kernel(count, orders, *refs):
-    number = len(orders)
-    refs = list(refs)
-
-    def take(size):
-        taken = refs[:size]
-        del refs[:size]
-        return taken
-
-    parts, (mod, rim) = take(number), take(2)
-    shares, (out_mod, out_rim) = take(number), take(2)
-    got1, got2, got3, got4 = take(number), take(number), take(number), take(number)
-    m1, m2, m3, m4 = take(4)
-    send, recv, send_far, recv_far = take(4)
-    groups = count // PLANE
-    me = lax.axis_index("seq")
-    bits = [lax.rem(me, 2), lax.rem(me // 2, 2), lax.rem(me // 4, 2)]
-    flips = [me + (1 - 2 * bits[i]) * (1 << i) for i in range(3)]
-    level = me // PLANE
-    low = lax.rem(me, PLANE)
-    left = lax.rem(me + count - 1, count)
-    right = lax.rem(me + 1, count)
-    far = [lax.rem(level + k, groups) for k in range(1, groups)]
-
-    barrier = pltpu.get_barrier_semaphore()
-    peers = flips + [left, right] + [g * PLANE + low for g in far]
-    for peer in peers:
-        pl.semaphore_signal(barrier, inc=1, device_id=(peer,), device_id_type=MESH)
-    pl.semaphore_wait(barrier, len(peers))
-
-    started = []
-
-    def push(src, dst, sems, slot, peer):
-        copy = pltpu.make_async_remote_copy(
-            src_ref=src,
-            dst_ref=dst,
-            send_sem=sems[0].at[slot],
-            recv_sem=sems[1].at[slot],
-            device_id=(peer,),
-            device_id_type=MESH,
-        )
-        copy.start()
-        started.append(copy)
-        return copy
-
-    near_sems, far_sems = (send, recv), (send_far, recv_far)
-
-    def near(src, dst, slot, peer):
-        return push(src, dst, near_sems, slot, peer)
-
-    def add(into, own, first):
-        def one(i, none):
-            into[i] = (into[i].astype(F32) + own[first + i].astype(F32)).astype(BF16)
-            return none
-
-        lax.fori_loop(0, into.shape[0], one, 0)
-
-    edges = [
-        near(rim.at[pl.ds(0, RIM)], out_rim.at[pl.ds(RIM, RIM)], 0, left),
-        near(rim.at[pl.ds(rim.shape[0] - RIM, RIM)], out_rim.at[pl.ds(0, RIM)], 1, right),
-    ]
-    base = 5
-    mods = near(mod, m1, 2, flips[0])
-    waits = [
-        near(parts[p].at[1 - bits[0]], got1[p], base + p, flips[0]) for p in range(number)
-    ]
-    half = 2 * groups
-    mods.wait_recv()
-    m1[...] += mod[...]
-    mods = near(m1, m2, 3, flips[1])
-    for p, order in enumerate(orders):
-        i = 1 if order == "xy" else 2
-        waits[p].wait_recv()
-        add(got1[p], parts[p].at[bits[0]], 0)
-        waits[p] = near(
-            got1[p].at[pl.ds((1 - bits[i]) * half, half)], got2[p], base + number + p, flips[i]
-        )
-    mods.wait_recv()
-    m2[...] += m1[...]
-    mods = near(m2, m3, 4, flips[2])
-    for p, order in enumerate(orders):
-        i, j = (1, 2) if order == "xy" else (2, 1)
-        waits[p].wait_recv()
-        add(got2[p], got1[p], bits[i] * half)
-        waits[p] = near(
-            got2[p].at[pl.ds((1 - bits[j]) * groups, groups)],
-            got3[p],
-            base + 2 * number + p,
-            flips[j],
-        )
-    mods.wait_recv()
-    m3[...] += m2[...]
-    last = []
-    for k, g in enumerate(far):
-        last.append(push(m3, m4.at[level], far_sems, k, g * PLANE + low))
-    m4[level] = m3[...]
-    for p, order in enumerate(orders):
-        j = 2 if order == "xy" else 1
-        waits[p].wait_recv()
-        add(got3[p], got2[p], bits[j] * groups)
-        for k, g in enumerate(far):
-            slot = (p + 1) * len(far) + k
-            last.append(push(got3[p].at[g], got4[p].at[level], far_sems, slot, g * PLANE + low))
-        got4[p][level] = got3[p][level]
-    for copy in last + edges:
-        copy.wait_recv()
-    for into, held in list(zip(shares, got4)) + [(out_mod, m4)]:
-        total = held[0].astype(F32)
-        for g in range(1, groups):
-            total = total + held[g].astype(F32)
-        into[...] = total
-    for copy in started:
-        copy.wait_send()
-
-
-def reduce_shares(parts, orders, mod, rim, count):
-    groups = count // PLANE
-    number = len(parts)
-    shapes = [part.shape[-2:] for part in parts]
-
-    def slots(size):
-        return [pltpu.VMEM((size,) + shape, BF16) for shape in shapes]
-
-    near = 5 + 3 * number
-    far = (number + 1) * (groups - 1)
-    return pl.pallas_call(
-        functools.partial(reduce_kernel, count, orders),
-        in_specs=[VMEM] * (number + 2),
-        out_specs=[VMEM] * (number + 2),
-        out_shape=[shaped(shape) for shape in shapes]
-        + [shaped(mod.shape), shaped((2 * RIM, rim.shape[1]))],
-        scratch_shapes=slots(4 * groups)
-        + slots(2 * groups)
-        + slots(groups)
-        + slots(groups)
-        + [pltpu.VMEM(mod.shape, F32)] * 3
-        + [pltpu.VMEM((groups,) + mod.shape, F32)]
-        + [pltpu.SemaphoreType.DMA((near,))] * 2
-        + [pltpu.SemaphoreType.DMA((far,))] * 2,
-        compiler_params=pltpu.CompilerParams(
-            collective_id=1, has_side_effects=True, vmem_limit_bytes=48 * MIB
-        ),
-        name="reduce_shares",
-    )(*parts, mod, rim)
+        *[given[name] for name in BLOCKED + FIXED],
+        slots_out,
+        slots_gate,
+        *[given[name] for name in FETCHED],
+    )
 
 
 def finish_kernel(
@@ -1356,12 +1535,18 @@
     output, gate_grad, gate_branch_grad, slots_out, slots_gate = run_mid(
         h, count, states_sum, d_skip, hidden, grad_out, w_out
     )
-    adjoint_side = run_adjoints(h, entering, kept)
-    norm_wide, mod_part, slots_a, slots_b = run_post(
-        h, count, adjoint_side, out_acc, (gate_grad, gate_branch_grad), d_skip, conv_w, w_x, w_dt, w_in
-    )
-    share_out, share_gate, share_a, share_b, mod, edges = reduce_shares(
-        (slots_out, slots_gate, slots_a, slots_b), ("xy", "yx", "xy", "yx"), mod_part, norm_wide, count
+    norm_wide, share_out, share_gate, share_a, share_b, mod, edges = run_back(
+        h,
+        count,
+        entering,
+        kept,
+        out_acc,
+        (gate_grad, gate_branch_grad, slots_out, slots_gate),
+        d_skip,
+        conv_w,
+        w_x,
+        w_dt,
+        w_in,
     )
     my_cond = lax.dynamic_slice_in_dim(condition, me * mrows, mrows, axis=1)
     results = pl.pallas_call(

time: 219 us -> 182 us (0.83)
  Pallas kernels: 189 us -> 154 us
    pallas_call x3 -> x1, Pallas kernels: 107 us -> 78.3 us  [run_back(): pl.pallas_call(functools.partial(back_kernel, count), grid=(inner // COLS...]
    pallas_call x1, Pallas kernels: 21.8 us -> 15.3 us  [run_states(): pl.pallas_call(states_kernel, grid=(inner // COLS,), in_specs=[s['both'],...]
    unnamed x51 -> x47, local copies, waits for them, and re-layouts: 20.6 us -> 19 us
where the time goes in v2:
time: 182 us; the launch traced here: 181 us
  Pallas kernels  154 us (85%)
  local copies, waits for them, and re-layouts  22.4 us (12%)
  starting transfers between devices  3.64 us (2%)
    pallas_call x1, Pallas kernels, run_back(): pl.pallas_call(functools.partial(back_kernel, count), grid=(inner // COLS...  78.3 us
    pallas_call x1, Pallas kernels, head(): pl.pallas_call(head_kernel, in_specs=[pl.BlockSpec(memory_space=pltpu.SME...  29.6 us
    pallas_call x1, Pallas kernels, carries(): pl.pallas_call(functools.partial(carry_kernel, count), in_specs=[VMEM, VM...  21 us
    unnamed x47, local copies, waits for them, and re-layouts  19 us
    pallas_call x1, Pallas kernels, run_states(): pl.pallas_call(states_kernel, grid=(inner // COLS,), in_specs=[s['both'],...  15.3 us
    pallas_call x1, Pallas kernels, run_mid(): pl.pallas_call(functools.partial(mid_kernel, count), in_specs=[VMEM] * 11...  8.34 us
  transfers between devices with their start and end apart: 2, of which 0 were waited for; matrix products, arithmetic and copies ran while one was open for 2% of the time, Pallas kernels for 0%

profile of v2, /device:TPU:0, one launch (start us, length us, event | category | flops | bytes accessed | tf_op | source)
XLA Modules:
  0.0 180.9 jit_solution(8197228506991303173)
XLA Ops:
  0.6 0.7 fusion
  1.4 2.3 %collective-permute-start = (bf16[8,768]{1,0:T(8,128)(2,1)S(1)}, bf16[8,768]{1,0:T(8,128)(2,1)S(1)}, u32[]{:S(2)}, u32[]{:S(2)}) collective-permute-start(bf16[8,768]{1,0:T(8,128)(2,1)S(1)} %get-tuple-element.120), channel_id=1, source_target_pairs={{0,1},{1,2},{2,3},{3,4},{4,5},{5,6},{6,7},{7,8},{8,9},{9,10},{10,1... | collective-permute-start | bytes 36872 | tf_op jit(solution)/shard_map/ppermute | solution.py:1517
  3.7 1.3 collective-permute-start.1
  5.0 0.8 constant_dynamic-slice_fusion.my_cond
  5.8 2.2 %copy.28.w_x_any.refs_18_ = bf16[2,1536,80]{2,1,0:T(8,128)(2,1)} copy(bf16[2,1536,80]{1,2,0:T(8,128)(2,1)} %param.23) | data formatting | bytes 983040 | tf_op args[8]
  8.0 1.3 reshape.33.b_mod
  9.3 0.6 copy-done.21
  9.9 0.6 copy-done.22
  10.5 29.6 %head.1 = (bf16[144,768]{1,0:T(8,128)(2,1)}, bf16[128,768]{1,0:T(8,128)(2,1)}, f32[144,768]{1,0:T(8,128)}, f32[128,128]{1,0:T(8,128)}, f32[128,768]{1,0:T(8,128)...) custom-call(s32[6]{0:T(128)} %lengths.1, ...), custom_call_target="tpu_custom_call" | custom-call | tf_op jit(solution)/shard_map/head/pallas_call | solution.py:378
  40.2 1.0 copy-done.10
  41.1 0.9 copy-done.12
  42.0 21.0 %carries.1 = bf16[24,2,16,128]{3,2,1,0:T(8,128)(2,1)S(1)} custom-call(bf16[24,3,16,128]{3,2,1,0:T(8,128)(2,1)S(1)} %copy-done.10, f32[24,16,128]{2,1,0:T(8,128)S(1)} %copy-done.12), custom_call_target="tpu_custom_call" | custom-call | tf_op jit(solution)/shard_map/carries/pallas_call | solution.py:541
  63.0 1.2 copy-done
  64.2 1.4 copy-done.1
  65.6 1.4 copy-done.2
  67.0 0.9 copy-done.6
  68.0 0.9 copy-done.15
  68.9 15.3 %states.1 = (f32[128,1536]{1,0:T(8,128)S(1)}, f32[2,128,256]{2,1,0:T(8,128)S(1)}, bf16[2,2064,1536]{2,1,0:T(8,128)(2,1)}) custom-call(f32[2,128,1536]{2,1,0:T(8,128)S(1)} %copy-done.1, f32[2,128,1536]{2,1,0:T(8,128)S(1)} %copy-done.2, f32[128,1536]{1,0:T(8,128)S(1)} %copy-done, f32[2,128,16,128]{3,2,1,0:T(8,128)} %get-tuple-element.69.in_spread, ...), custom_call_target="tpu_custom_call" | custom-call | tf_op jit(solution)/shard_map/states/pallas_call | solution.py:651
  84.2 0.9 copy-done.7
  85.1 0.7 copy-done.11
  85.8 8.3 %mid.1 = (bf16[128,768]{1,0:T(8,128)(2,1)}, f32[128,768]{1,0:T(8,128)}, bf16[128,1536]{1,0:T(8,128)(2,1)}, bf16[2,16,48,768]{3,2,1,0:T(8,128)(2,1)}, bf16[2,16,48,768]{3,2,1,0:T(8,128)(2,1)}) custom-call(f32[128,1536]{1,0:T(8,128)} %copy-done.7, bf16[2,128,1536]{2,1,0:T(8,128)(2,1)} %get-tuple-element.75.active.refs_16_, f32[2,1536]{1,0:T(2,128)} %refs_8_.1, ...), custom_call_target="tpu_custom_call" | custom-call | tf_op jit(solution)/shard_map/mid/pallas_call | solution.py:749
  94.1 0.0 copy-start.9
  94.2 78.3 %back.1 = (f32[144,768]{1,0:T(8,128)}, f32[48,768]{1,0:T(8,128)}, f32[48,768]{1,0:T(8,128)}, f32[48,512]{1,0:T(8,128)}, f32[48,640]{1,0:T(8,128)}, /*index=5*/f32[8,2304]{1,0:T(8,128)}, f32[16,768]{1,0:T(8,128)}) custom-call(f32[2,128,1536]{2,1,0:T(8,128)} %get-tuple-element.66.masked.refs_0_, f32[2,128,1536]{2,1,0:T(8,128)} %get-tuple-element.67.driven.refs_1_, ...), custom_call_target="tpu_custom_call" | custom-call | tf_op jit(solution)/shard_map/back/pallas_call | solution.py:1375
  172.5 1.0 copy-done.8
  173.5 0.9 copy-done.13
  174.5 0.9 copy-done.14
  175.4 0.9 copy-done.16
  176.3 0.9 copy-done.17
  177.2 0.9 copy-done.18
  178.0 0.8 copy-done.20
  178.8 1.4 finish.1
  180.3 0.6 dynamic-slice_bitcast_fusion
  (29 shorter events, 0.1 us)
Async XLA Ops:
  1.4 7.9 %collective-permute-start = (bf16[8,768]{1,0:T(8,128)(2,1)S(1)}, bf16[8,768]{1,0:T(8,128)(2,1)S(1)}, u32[]{:S(2)}, u32[]{:S(2)}) collective-permute-start(bf16[8,768]{1,0:T(8,128)(2,1)S(1)} %get-tuple-element.120), channel_id=1, source_target_pairs={{0,1},{1,2},{2,3},{3,4},{4,5},{5,6},{6,7},{7,8},{8,9},{9,10},{10,1... | collective-permute-start | bytes 36872 | tf_op jit(solution)/shard_map/ppermute | solution.py:1517
  3.7 5.6 %collective-permute-start.1 = (bf16[8,768]{1,0:T(8,128)(2,1)S(1)}, bf16[8,768]{1,0:T(8,128)(2,1)S(1)}, u32[]{:S(2)}, u32[]{:S(2)}) collective-permute-start(bf16[8,768]{1,0:T(8,128)(2,1)S(1)} %get-tuple-element.119), channel_id=1, source_target_pairs={{1,0},{2,1},{3,2},{4,3},{5,4},{6,5},{7,6},{8,7},{9,8},{10,9},{11,1... | collective-permute-start | bytes 36872 | tf_op jit(solution)/shard_map/ppermute | solution.py:1518
  9.3 0.6 copy-start.21
  9.9 0.6 copy-start.22
  40.1 1.0 copy-start.10
  41.1 0.9 copy-start.12
  63.0 21.2 %copy-start.4 = (bf16[24,2,16,128]{3,2,1,0:T(8,128)(2,1)}, bf16[24,2,16,128]{3,2,1,0:T(8,128)(2,1)S(1)}, u32[]{:S(2)}) copy-start(bf16[24,2,16,128]{3,2,1,0:T(8,128)(2,1)S(1)} %carries.1) | copy-start | bytes 589828
  63.0 1.2 copy-start
  64.2 1.4 copy-start.1
  65.6 1.4 copy-start.2
  67.0 0.9 copy-start.6
  68.0 0.9 copy-start.15
  84.2 0.9 copy-start.7
  85.1 0.7 copy-start.11
  94.1 78.4 %copy-start.3 = (f32[144,768]{1,0:T(8,128)S(1)}, f32[144,768]{1,0:T(8,128)}, u32[]{:S(2)}) copy-start(f32[144,768]{1,0:T(8,128)} %get-tuple-element.96.refs_26_.normed) | copy-start | bytes 1327108
  94.1 78.4 %copy-start.5 = (bf16[128,768]{1,0:T(8,128)(2,1)S(1)}, bf16[128,768]{1,0:T(8,128)(2,1)}, u32[]{:S(2)}) copy-start(bf16[128,768]{1,0:T(8,128)(2,1)} %grad_out.5) | copy-start | bytes 589828
  94.1 78.4 %copy-start.9 = (f32[128,768]{1,0:T(8,128)S(1)}, f32[128,768]{1,0:T(8,128)}, u32[]{:S(2)}) copy-start(f32[128,768]{1,0:T(8,128)} %get-tuple-element.106.scale1) | copy-start | bytes 1179652
  94.2 78.4 %copy-start.19 = (f32[128,128]{1,0:T(8,128)S(1)}, f32[128,128]{1,0:T(8,128)}, u32[]{:S(2)}) copy-start(f32[128,128]{1,0:T(8,128)} %get-tuple-element.105.rescale) | copy-start | bytes 196612
  172.5 1.0 copy-start.8
  173.5 0.9 copy-start.13
  174.4 0.9 copy-start.14
  175.4 0.9 copy-start.16
  176.3 0.9 copy-start.17
  177.2 0.9 copy-start.18
  178.0 0.8 copy-start.20
